TPU v7x, 32 devices: a whole 2x2x4 slice. The times are simulated.
32 devices in a mesh: seq: 4 (over z), head: 8 (over y, x, core).
Axes of the slice: x: 2, y: 2, z: 4, core: 2. Of those that a mesh axis runs over, the one named last changes fastest.
Arguments:
- x_in: bfloat16 [4096, 16384], P('seq', 'head'), may hold values from -40 to 40
- z_gate: bfloat16 [4096, 16384], P('seq', 'head'), may hold values from -6 to 6
- b_input: bfloat16 [4096, 8, 128], P('seq'), may hold values from -2 to 2
- c_input: bfloat16 [4096, 8, 128], P('seq'), may hold values from -2 to 2
- dt_raw: float32 [128, 4096], P('head', 'seq'), may hold values from -5 to 1366
- a_log: float32 [128], P('head'), may hold values from -20 to 0
- d_skip: float32 [128], P('head'), may hold values from 0.5 to 2
- norm_gain: float32 [16384], P('head'), may hold values from 0.25 to 1.75
- doc_lengths: int32 [6], replicated, may hold values from 1 to 1365, 4096 in all
- doc_lang: int32 [6], replicated, may hold values from 0 to 3
- adapt_down: bfloat16 [4, 16384, 128], P(None, 'head'), may hold values from -0.046875 to 0.046875
- adapt_up: bfloat16 [4, 128, 16384], P(None, None, 'head'), may hold values from -0.5 to 0.5
Outputs:
- adapted: bfloat16 [4096, 16384], P('seq', 'head')
Inputs may be any that keep to these rules, and one draw needn't show every extreme that they name: `doc_lengths`: the lengths sum to 4096; the longest document has exactly 1365 tokens.
All inputs are finite; a program needn't handle non-finite values.
Results may differ from a plain program's by a relative error of at most 0.0075.
Values may be sent and summed in bfloat16 or wider, within the bound.
No kernel may reach another device: no remote copies, remote signals or barrier semaphores. Data moves between devices by JAX's collectives and lax.ppermute only.
A program may use at most 128 MiB of HBM per device.

v0:
```python
import jax
import jax.numpy as jnp
from jax import lax
from jax.sharding import PartitionSpec as P

SPACE_HEADS = 128
HEAD_DIM = 128
GROUPS = 8


highest = lax.Precision.HIGHEST


def doc_tables(doc_lengths, doc_lang, token_positions, lang_count):
    doc_ends = jnp.cumsum(doc_lengths)
    doc_start = doc_ends - doc_lengths
    doc_index = (
        jnp.sum((token_positions[:, None] >= doc_start[None, :]).astype(jnp.int32), axis=1) - 1
    )
    is_first = jnp.sum((token_positions[:, None] == doc_start[None, :]).astype(jnp.int32), axis=1)
    doc_hot = (
        doc_index[:, None] == jnp.arange(doc_lengths.shape[0], dtype=jnp.int32)[None, :]
    ).astype(jnp.int32)
    lang_index = jnp.sum(doc_hot * doc_lang[None, :], axis=1)
    lang_hot = lang_index[:, None] == jnp.arange(lang_count, dtype=jnp.int32)[None, :]
    return (doc_index, is_first, lang_hot)


def block_scan(x_vals, step_dt, log_decay, b_vals, c_vals, doc_index, is_first):
    head_count, length, head_width = x_vals.shape
    states = b_vals.shape[1]
    block_len = min(128, length)
    block_count = length // block_len
    x_blocks = x_vals.reshape(head_count, block_count, block_len, head_width).transpose(1, 0, 2, 3)
    dt_blocks = step_dt.reshape(head_count, block_count, block_len).transpose(1, 0, 2)
    dec_blocks = log_decay.reshape(head_count, block_count, block_len).transpose(1, 0, 2)
    b_blocks = b_vals.reshape(block_count, block_len, states)
    c_blocks = c_vals.reshape(block_count, block_len, states)
    doc_blocks = doc_index.reshape(block_count, block_len)
    first_blocks = is_first.reshape(block_count, block_len)
    lower_mask = jnp.arange(block_len)[:, None] >= jnp.arange(block_len)[None, :]

    def advance(carry_state, pieces):
        x_block, dt_block, dec_block, b_block, c_block, doc_block, first_block = pieces
        cumulative = jnp.cumsum(dec_block, axis=1)
        keep_mask = lower_mask & (doc_block[:, None] == doc_block[None, :])
        decay_gaps = jnp.where(
            keep_mask[None], cumulative[:, :, None] - cumulative[:, None, :], 0.0
        )
        scores = jnp.dot(c_block, b_block.T, preferred_element_type=jnp.float32)
        weights = (
            jnp.where(keep_mask[None], jnp.exp(decay_gaps), 0.0)
            * scores[None]
            * dt_block[:, None, :]
        )
        x_float = x_block.astype(jnp.float32)
        inner_part = jnp.einsum("hij,hjp->hip", weights, x_float, precision=highest)
        reach_mask = (jnp.cumsum(first_block) == 0).astype(jnp.float32)
        carried = jnp.einsum(
            "in,hnp->hip", c_block.astype(jnp.float32), carry_state, precision=highest
        )
        carried = carried * (jnp.exp(cumulative) * reach_mask[None])[:, :, None]
        tail_keep = doc_block == doc_block[-1]
        tail_gaps = jnp.where(tail_keep[None], cumulative[:, -1:] - cumulative, 0.0)
        fresh_weight = jnp.where(tail_keep[None], jnp.exp(tail_gaps), 0.0) * dt_block
        written = jnp.einsum(
            "jn,hjp->hnp",
            b_block.astype(jnp.float32),
            x_float * fresh_weight[:, :, None],
            precision=highest,
        )
        kept_share = jnp.exp(cumulative[:, -1]) * reach_mask[-1]
        return (carry_state * kept_share[:, None, None] + written, inner_part + carried)

    initial = jnp.zeros((head_count, states, head_width), jnp.float32)
    final_state, outputs = lax.scan(
        advance,
        initial,
        (x_blocks, dt_blocks, dec_blocks, b_blocks, c_blocks, doc_blocks, first_blocks),
    )
    outputs = outputs.transpose(1, 0, 2, 3).reshape(head_count, length, head_width)
    return (outputs, final_state)


def per_device(
    x_in,
    z_gate,
    b_input,
    c_input,
    dt_raw,
    a_log,
    d_skip,
    norm_gain,
    doc_lengths,
    doc_lang,
    adapt_down,
    adapt_up,
):
    tok_local = x_in.shape[0]
    head_local = dt_raw.shape[0]
    head_width = x_in.shape[1] // head_local
    seq_rank = lax.axis_index("seq")
    head_rank = lax.axis_index("head")
    token_positions = seq_rank * tok_local + jnp.arange(tok_local, dtype=jnp.int32)
    doc_index, is_first, lang_hot = doc_tables(
        doc_lengths, doc_lang, token_positions, adapt_down.shape[0]
    )
    group_index = head_rank * head_local // (SPACE_HEADS // GROUPS)
    b_local = lax.dynamic_index_in_dim(b_input, group_index, axis=1, keepdims=False)
    c_local = lax.dynamic_index_in_dim(c_input, group_index, axis=1, keepdims=False)
    step_dt = jax.nn.softplus(dt_raw)
    log_decay = step_dt * (-jnp.exp(a_log))[:, None]
    x_heads = x_in.reshape(tok_local, head_local, head_width).transpose(1, 0, 2)
    local_out, local_state = block_scan(
        x_heads, step_dt, log_decay, b_local, c_local, doc_index, is_first
    )
    cumulative = jnp.cumsum(log_decay, axis=1)
    reach_mask = (jnp.cumsum(is_first) == 0).astype(jnp.float32)
    through = jnp.exp(cumulative[:, -1]) * reach_mask[-1]
    all_through = lax.all_gather(through[None], "seq", axis=0, tiled=True)
    shard_ids = jnp.arange(all_through.shape[0], dtype=jnp.int32)
    shards = lax.all_gather(local_state[None], "seq", axis=0, tiled=True)
    sources = jnp.arange(shards.shape[0], dtype=jnp.int32)
    between = (shard_ids[None, :] > sources[:, None]) & (shard_ids[None, :] < seq_rank)
    factors = jnp.prod(jnp.where(between[:, :, None], all_through[None], 1.0), axis=1)
    factors = factors * (sources < seq_rank).astype(jnp.float32)[:, None]
    incoming = jnp.einsum("mh,mhnp->hnp", factors, shards, precision=highest)
    entering = jnp.einsum("ln,hnp->hlp", c_local.astype(jnp.float32), incoming, precision=highest)
    entering = entering * (jnp.exp(cumulative) * reach_mask[None])[:, :, None]
    ssd_heads = local_out + entering + d_skip[:, None, None] * x_heads.astype(jnp.float32)
    ssd_rows = ssd_heads.transpose(1, 0, 2).reshape(tok_local, head_local * head_width)
    gated = ssd_rows * jax.nn.silu(z_gate.astype(jnp.float32))
    square_sum = lax.psum(jnp.sum(gated * gated, axis=1), "head")
    mean_square = square_sum / (SPACE_HEADS * HEAD_DIM)
    normed = (gated * lax.rsqrt(mean_square + 1e-05)[:, None] * norm_gain[None, :]).astype(
        jnp.bfloat16
    )
    partial_value = jnp.einsum(
        "td,kdr->tkr", normed, adapt_down, preferred_element_type=jnp.float32
    )
    picked = jnp.sum(jnp.where(lang_hot[:, :, None], partial_value, 0.0), axis=1)
    low_rank = lax.psum(picked, "head").astype(jnp.bfloat16)
    selected = jnp.where(lang_hot[:, :, None], low_rank[:, None, :], jnp.zeros((), jnp.bfloat16))
    selected = selected.reshape(tok_local, adapt_up.shape[0] * adapt_up.shape[1])
    lifted = jnp.dot(
        selected,
        adapt_up.reshape(adapt_up.shape[0] * adapt_up.shape[1], adapt_up.shape[2]),
        preferred_element_type=jnp.float32,
    )
    return (normed.astype(jnp.float32) + lifted).astype(jnp.bfloat16)


def solution(mesh):
    placed = (
        P("seq", "head"),
        P("seq", "head"),
        P("seq", None, None),
        P("seq", None, None),
        P("head", "seq"),
        P("head"),
        P("head"),
        P("head"),
        P(),
        P(),
        P(None, "head", None),
        P(None, None, "head"),
    )
    return jax.shard_map(
        per_device, mesh=mesh, in_specs=placed, out_specs=P("seq", "head"), check_vma=False
    )
```

profile of v0, /device:TPU:0, one launch (start us, length us, event | category | flops | bytes accessed | tf_op | source)
XLA Modules:
  0.0 343.5 jit_solution(4890242331479904555)
XLA Ops:
  6.5 3.5 %constant_dynamic-slice_fusion.4 = (bf16[1024,1,128]{2,1,0:T(2,128)(2,1)S(1)}, bf16[1024,1,128]{2,1,0:T(2,128)(2,1)S(1)}) fusion(bf16[1024,8,128]{2,1,0:T(8,128)(2,1)} %param.17, s32[]{:T(128)S(6)} %select_n.50, bf16[1024,8,128]{2,1,0:T(8,128)(2,1)} %param.16), kind=kLoop, calls=%fused_computation.108 | loop fusion | bytes 1048580 | tf_op jit(solution)/shard_map/jit(dynamic_index_in_dim)/dynamic_slice | solution.py:110
  15.8 6.4 %copy.56 = bf16[1024,2048]{0,1:T(8,128)(2,1)} copy(bf16[1024,2048]{1,0:T(8,128)(2,1)} %param.14) | data formatting | bytes 8388608 | tf_op args[0]
  22.2 5.4 %copy.92 = bf16[16,16,8,8,128]{4,3,1,0,2:T(8,128)(2,1)} copy(bf16[16,16,8,8,128]{4,3,2,1,0:T(8,128)(2,1)} %bitcast.154) | data formatting | bytes 8388608 | tf_op jit(solution)/shard_map/reshape | solution.py:34
  28.2 137.4 %while.13 = (s32[]{:T(128)}, f32[16,128,128]{1,2,0:T(8,128)S(1)}, f32[8,16,128,128]{3,2,1,0:T(8,128)}, f32[8,16,128]{2,0,1:T(8,128)}, s32[8,128]{1,0:T(8,128)}, ...) while((s32[]{:T(128)}, f32[16,128,128]{1,2,0:T(8,128)S(1)}, ...), condition=%wide.region_6.7_spmd.clone, body=%wide.region_3.0_spmd.clone.sunk | while | flops 1215898112 | bytes 7802700 | solution.py:76
  31.0 3.4 fusion.98
  38.2 3.0 fusion.99
  48.2 3.4 fusion.98
  55.4 3.0 fusion.99
  65.4 3.4 fusion.98
  72.6 3.0 fusion.99
  82.6 3.4 fusion.98
  89.8 3.0 fusion.99
  99.8 3.4 fusion.98
  106.9 3.0 fusion.99
  116.9 3.4 fusion.98
  124.1 3.0 fusion.99
  134.1 3.4 fusion.98
  141.3 3.0 fusion.99
  151.3 3.4 fusion.98
  158.5 3.0 fusion.99
  167.9 9.3 %copy.62 = f32[16,8,128,128]{2,1,3,0:T(8,128)} copy(f32[16,8,128,128]{3,2,0,1:T(8,128)} %bitcast.158) | data formatting | bytes 16777216 | tf_op jit(solution)/shard_map/transpose | solution.py:81
  177.2 9.5 %reshape.358 = f32[16,1024,128]{1,2,0:T(8,128)} reshape(f32[16,8,128,128]{2,1,3,0:T(8,128)} %copy.62) | data formatting | bytes 16777216 | tf_op jit(solution)/shard_map/reshape | solution.py:81
  187.6 4.5 %reduce-window.38 = f32[16,8,128]{2,1,0:T(8,128)S(1)} reduce-window(f32[16,8,128]{2,1,0:T(8,128)S(1)} %bitcast.169, f32[]{:T(128)} %constant.78.clone.1), window={size=1x1x128 pad=0_0x0_0x127_0}, to_apply=%region_7.8 | reduce-window | flops 2080768 | bytes 131076 | tf_op jit(solution)/shard_map/reduce-window.2
  194.7 13.9 %all-reduce = f32[64]{0:T(128)S(1)} all-reduce(f32[64]{0:T(128)S(1)} %bitcast_dynamic-update-slice_fusion), channel_id=2, replica_groups=mesh['seq'=4,'head'=8] {'seq'}, use_global_device_ids=true, to_apply=%add | all-reduce | flops 64 | bytes 512
  208.9 41.8 %all-gather.4.cloned.1.call-done = f32[64,128,128]{2,1,0:T(8,128)} async-done(((f32[16,128,128]{2,1,0:T(8,128)}), f32[64,128,128]{2,1,0:T(8,128)}) %all-gather.4.cloned.1.call-update) | async-done | bytes 4194320 | tf_op jit(solution)/shard_map/all_gather | solution.py:122
  253.4 9.9 %fusion.53 = f32[16,1024,128]{1,2,0:T(8,128)} fusion(f32[16,1024,128]{1,2,0:T(8,128)} %reshape.358, bf16[16,1024,128]{1,2,0:T(8,128)(2,1)} %bitcast.155, f32[16]{0:T(128)S(1)} %copy-done.4, f32[16,1024]{1,0:T(8,128)S(1)} %exponential_multiply_fusion.2, f32[16,128,128]{2,1,0:T(8,128)S(1)} %multiply_reduce_fusion.1, bf16[1024,1,128]{2,0,1:T(8,128)(2,1)S(1)} %bitcast.161), kind=kOutput, calls=%fused_computation.69 | convolution fusion | flops 3231711232 | bytes 22347840 | tf_op jit(solution)/shard_map/ln,hnp->hlp/dot_general | solution.py:128
  263.4 9.1 %copy.67 = f32[1024,2048]{1,0:T(8,128)} copy(f32[1024,2048]{0,1:T(8,128)} %bitcast.156) | data formatting | bytes 16777216 | tf_op jit(solution)/shard_map/reshape | solution.py:131
  272.5 9.0 %multiply_reduce_fusion = (f32[1024]{0:T(1024)S(1)}, f32[1024,2048]{1,0:T(8,128)}) fusion(f32[1024,2048]{1,0:T(8,128)} %copy.67, bf16[1024,2048]{1,0:T(8,128)(2,1)} %param.15), kind=kLoop, calls=%fused_computation.71 | loop fusion | flops 16776192 | bytes 20975616 | tf_op jit(solution)/shard_map/reduce_sum | solution.py:133
  281.4 13.6 %psum.14 = f32[1024]{0:T(1024)S(1)} all-reduce(f32[1024]{0:T(1024)S(1)} %get-tuple-element.152), channel_id=1, replica_groups=mesh['seq'=4,'head'=8] {'head'}, use_global_device_ids=true, to_apply=%region_13.14 | all-reduce | flops 1024 | bytes 8192 | tf_op jit(solution)/shard_map/psum | solution.py:133
  295.1 5.7 %select_reduce_fusion = f32[1024,128]{1,0:T(8,128)S(1)} fusion(bf16[4,2048,128]{2,1,0:T(8,128)(2,1)} %param.24, pred[1024,4]{0,1:T(4,128)(4,1)S(1)} %iota_compare_fusion.2, f32[1024,2048]{1,0:T(8,128)} %get-tuple-element.153, f32[2048]{0:T(1024)S(1)} %copy-done.6, f32[1024]{0:T(1024)S(1)} %add_rsqrt_fusion), kind=kOutput, calls=%fused_computation.76 | convolution fusion | flops 2154692608 | bytes 11026432 | tf_op jit(solution)/shard_map/td,kdr->tkr/dot_general | solution.py:138
  300.8 29.7 %all-reduce.2 = bf16[1024,128]{1,0:T(8,128)(2,1)S(1)} all-reduce(f32[1024,128]{1,0:T(8,128)S(1)} %select_reduce_fusion), channel_id=1, replica_groups=mesh['seq'=4,'head'=8] {'head'}, use_global_device_ids=true, to_apply=%region_16.17 | all-reduce | flops 131072 | bytes 786432 | tf_op jit(solution)/shard_map/psum | solution.py:142
  330.5 6.2 %fusion.52 = bf16[1024,2048]{1,0:T(8,128)(2,1)} fusion(bf16[4,128,2048]{2,1,0:T(8,128)(2,1)S(1)} %copy-done, pred[1024,4]{0,1:T(4,128)(4,1)S(1)} %iota_compare_fusion.2, bf16[1024,128]{1,0:T(8,128)(2,1)S(1)} %all-reduce.2, f32[2048]{0:T(1024)S(1)} %copy-done.6, f32[1024,2048]{1,0:T(8,128)} %get-tuple-element.153, f32[1024]{0:T(1024)S(1)} %add_rsqrt_fusion), kind=kOutput, calls=%fused_computation.67 | convolution fusion | flops 2160590848 | bytes 14958592 | tf_op jit(solution)/shard_map/dot_general | solution.py:145
  (203 shorter events, 100.4 us)
Async XLA Ops:
  6.5 323.9 %copy-start = (bf16[4,128,2048]{2,1,0:T(8,128)(2,1)S(1)}, bf16[4,128,2048]{2,1,0:T(8,128)(2,1)}, u32[]{:S(2)}) copy-start(bf16[4,128,2048]{2,1,0:T(8,128)(2,1)} %param.25) | copy-start | bytes 6291460
  6.5 244.2 %all-gather.4.cloned.1.call-start = ((), (), s32[]{:S(2)}) async-start(), calls=%async_computation | async-start | bytes 5242880 | tf_op jit(solution)/shard_map/all_gather | solution.py:122
  29.1 8.0 %copy-start.1 = (f32[1,16,128]{2,0,1:T(1,128)}, f32[1,16,128]{2,0,1:T(1,128)S(1)}, u32[]{:S(2)}) copy-start(f32[1,16,128]{2,0,1:T(1,128)S(1)} %get-tuple-element.235) | copy-start | bytes 24580 | tf_op jit(solution)/shard_map/while
  46.2 8.0 %copy-start.1 = (f32[1,16,128]{2,0,1:T(1,128)}, f32[1,16,128]{2,0,1:T(1,128)S(1)}, u32[]{:S(2)}) copy-start(f32[1,16,128]{2,0,1:T(1,128)S(1)} %get-tuple-element.235) | copy-start | bytes 24580 | tf_op jit(solution)/shard_map/while
  63.4 8.0 %copy-start.1 = (f32[1,16,128]{2,0,1:T(1,128)}, f32[1,16,128]{2,0,1:T(1,128)S(1)}, u32[]{:S(2)}) copy-start(f32[1,16,128]{2,0,1:T(1,128)S(1)} %get-tuple-element.235) | copy-start | bytes 24580 | tf_op jit(solution)/shard_map/while
  80.6 8.0 %copy-start.1 = (f32[1,16,128]{2,0,1:T(1,128)}, f32[1,16,128]{2,0,1:T(1,128)S(1)}, u32[]{:S(2)}) copy-start(f32[1,16,128]{2,0,1:T(1,128)S(1)} %get-tuple-element.235) | copy-start | bytes 24580 | tf_op jit(solution)/shard_map/while
  97.8 8.0 %copy-start.1 = (f32[1,16,128]{2,0,1:T(1,128)}, f32[1,16,128]{2,0,1:T(1,128)S(1)}, u32[]{:S(2)}) copy-start(f32[1,16,128]{2,0,1:T(1,128)S(1)} %get-tuple-element.235) | copy-start | bytes 24580 | tf_op jit(solution)/shard_map/while
  114.9 8.0 %copy-start.1 = (f32[1,16,128]{2,0,1:T(1,128)}, f32[1,16,128]{2,0,1:T(1,128)S(1)}, u32[]{:S(2)}) copy-start(f32[1,16,128]{2,0,1:T(1,128)S(1)} %get-tuple-element.235) | copy-start | bytes 24580 | tf_op jit(solution)/shard_map/while
  132.1 8.0 %copy-start.1 = (f32[1,16,128]{2,0,1:T(1,128)}, f32[1,16,128]{2,0,1:T(1,128)S(1)}, u32[]{:S(2)}) copy-start(f32[1,16,128]{2,0,1:T(1,128)S(1)} %get-tuple-element.235) | copy-start | bytes 24580 | tf_op jit(solution)/shard_map/while
  149.3 8.0 %copy-start.1 = (f32[1,16,128]{2,0,1:T(1,128)}, f32[1,16,128]{2,0,1:T(1,128)S(1)}, u32[]{:S(2)}) copy-start(f32[1,16,128]{2,0,1:T(1,128)S(1)} %get-tuple-element.235) | copy-start | bytes 24580 | tf_op jit(solution)/shard_map/while
  177.2 10.4 %copy-start.2 = (f32[8,16,128]{2,0,1:T(8,128)S(1)}, f32[8,16,128]{2,0,1:T(8,128)}, u32[]{:S(2)}) copy-start(f32[8,16,128]{2,0,1:T(8,128)} %get-tuple-element.283) | copy-start | bytes 196612
  177.2 16.1 %copy-start.7 = (u32[32]{0:T(128)S(1)}, u32[32]{0:T(128)}, u32[]{:S(2)}) copy-start(u32[32]{0:T(128)} %constant.94) | copy-start | bytes 388
  177.2 31.5 %copy-start.3 = (s32[1024]{0:T(1024)S(1)}, s32[1024]{0:T(1024)}, u32[]{:S(2)}) copy-start(s32[1024]{0:T(1024)} %get-tuple-element.163) | copy-start | bytes 12292
  177.2 31.5 %copy-start.5 = (s32[6]{0:T(128)S(1)}, s32[6]{0:T(128)}, u32[]{:S(2)}) copy-start(s32[6]{0:T(128)} %param.23) | copy-start | bytes 76
  177.2 76.2 %copy-start.4 = (f32[16]{0:T(128)S(1)}, f32[16]{0:T(128)}, u32[]{:S(2)}) copy-start(f32[16]{0:T(128)} %param.20) | copy-start | bytes 196
  272.5 22.6 %copy-start.6 = (f32[2048]{0:T(1024)S(1)}, f32[2048]{0:T(1024)}, u32[]{:S(2)}) copy-start(f32[2048]{0:T(1024)} %param.21) | copy-start | bytes 24580
Sparse Core Ops, SparseCore 0:
  167.1 83.6 all-gather.3
where the time goes:
time: 347 us; the launch traced here: 344 us
  matrix products  98.2 us (28%)
  local copies, waits for them, and re-layouts  77.5 us (22%)
  blocking collectives  57.2 us (16%)
  other arithmetic  54.2 us (16%)
  waiting for transfers between devices  41.8 us (12%)
  between operations  14.2 us (4%)
    all_gather x1, waiting for transfers between devices, per_device(): shards = lax.all_gather(local_state[None], 'seq', axis=0, tiled=True)  41.8 us
    psum x1, blocking collectives, per_device(): low_rank = lax.psum(picked, 'head').astype(jnp.bfloat16)  29.7 us
    dot_general x8, matrix products, advance(): inner_part = jnp.einsum('hij,hjp->hip', weights, x_float, precision=highest)  27.2 us
    dot_general x8, matrix products, advance(): jnp.einsum('in,hnp->hip', c_block.astype(jnp.float32), carry_state, preci...  23.9 us
    dot_general x8, matrix products, advance(): jnp.einsum('jn,hjp->hnp', b_block.astype(jnp.float32), x_float * fresh_we...  18.1 us
    unnamed x1, blocking collectives  13.9 us
    psum x1, blocking collectives, per_device(): square_sum = lax.psum(jnp.sum(gated * gated, axis=1), 'head')  13.6 us
    dynamic_slice x16, local copies, waits for them, and re-layouts, block_scan(): lax.scan(advance, initial, (x_blocks, dt_blocks, dec_blocks, b_blocks, c_...  12.6 us
  transfers between devices with their start and end apart: 1, of which 1 were waited for; matrix products, arithmetic and copies ran while one was open for 8% of the time, Pallas kernels for 0%

commit v1 on v0

v1 whole, which is shorter than its diff:
```python
import functools

import jax
import jax.numpy as jnp
from jax import lax
from jax.experimental import pallas as pl
from jax.experimental.pallas import tpu as pltpu
from jax.sharding import PartitionSpec as P

F32 = jnp.float32
BF16 = jnp.bfloat16
I32 = jnp.int32
LOG2E = 1.4426950408889634
EPS = 1e-05
LANES = 128
SUM_ROWS = 16
LONGEST_SHARE = 3
VMEM_LIMIT = 48 * 1024 * 1024


def params():
    return pltpu.CompilerParams(vmem_limit_bytes=VMEM_LIMIT)


def starts_of(len_ref):
    starts, at = [], jnp.int32(0)
    for d in range(len_ref.shape[0]):
        starts.append(at)
        at = at + len_ref[d]
    return starts


def doc_at(pos, starts):
    found = jnp.where(pos >= starts[0], 0, -1)
    for s in starts[1:]:
        found = found + jnp.where(pos >= s, 1, 0)
    return found


def lang_at(pos, starts, lang_ref):
    found = jnp.where(pos >= 0, lang_ref[0], 0)
    for d in range(1, len(starts)):
        found = jnp.where(pos >= starts[d], lang_ref[d], found)
    return found


def rates(alog_ref, rows):
    which = lax.broadcasted_iota(I32, (rows, LANES), 0)
    column = jnp.zeros((rows, LANES), F32)
    for h in range(rows):
        column = jnp.where(which == h, alog_ref[h], column)
    return -LOG2E * jnp.exp(column)


def softplus(v):
    return jnp.maximum(v, 0.0) + jnp.log(1.0 + jnp.exp(-jnp.abs(v)))


def running(v, back):
    width = v.shape[1]
    lane = lax.broadcasted_iota(I32, v.shape, 1)
    step = 1
    while step < width:
        if back:
            v = v + jnp.where(lane + step < width, pltpu.roll(v, width - step, 1), 0.0)
        else:
            v = v + jnp.where(lane >= step, pltpu.roll(v, step, 1), 0.0)
        step *= 2
    return v


def pick_matrix(group, groups):
    shape = (LANES, LANES * groups)
    row = lax.broadcasted_iota(I32, shape, 0)
    col = lax.broadcasted_iota(I32, shape, 1)
    return jnp.where(col == row * groups + group, 1.0, 0.0).astype(BF16)


def dot(a, b):
    return jnp.dot(a, b, preferred_element_type=F32)


def state_kernel(heads_per, meta, len_ref, alog_ref, dt_ref, b_ref, x_ref, state_ref, thr_ref, bsel_ref, bt_ref, w_ref, all_ref):
    step = pl.program_id(0)
    heads, tokens = dt_ref.shape
    groups = b_ref.shape[0] // tokens

    @pl.when(step == 0)
    def _():
        pick = pick_matrix(meta[1], groups)
        for c in range(tokens // LANES):
            here = slice(c * LANES, (c + 1) * LANES)
            chosen = dot(pick, b_ref[c * LANES * groups:(c + 1) * LANES * groups, :])
            bsel_ref[here, :] = chosen.astype(BF16)
            bt_ref[:, here] = chosen.T
        starts = starts_of(len_ref)
        base = meta[0]
        rate = rates(alog_ref, heads)
        parts, totals = [], []
        for c in range(tokens // LANES):
            step_dt = softplus(dt_ref[:, c * LANES:(c + 1) * LANES])
            decay = step_dt * rate
            after = running(decay, True)
            parts.append((step_dt, after - decay))
            totals.append(after[:, 0:1])
        last_doc = doc_at(base + tokens - 1, starts)
        first_doc = doc_at(base - 1, starts)
        later = jnp.zeros((heads, 1), F32)
        for c in reversed(range(tokens // LANES)):
            step_dt, inside = parts[c]
            pos = base + c * LANES + lax.broadcasted_iota(I32, (heads, LANES), 1)
            alive = doc_at(pos, starts) == last_doc
            w_ref[:, c * LANES:(c + 1) * LANES] = jnp.where(alive, jnp.exp2(inside + later) * step_dt, 0.0)
            later = later + totals[c]
        kept = jnp.where(last_doc == first_doc, 1.0, 0.0)
        all_ref[...] = jnp.broadcast_to(jnp.exp2(later) * kept, all_ref.shape)

    for i in range(heads_per):
        h = step * heads_per + i
        here = slice(i * LANES, (i + 1) * LANES)
        weighted = (bt_ref[...] * w_ref[pl.ds(h, 1), :]).astype(BF16)
        state_ref[:, here] = dot(weighted, x_ref[:, here]).astype(BF16)
        thr_ref[:, here] = jnp.broadcast_to(all_ref[pl.ds(h, 1), :], (8, LANES))


def block_states(meta, doc_lengths, a_log, dt_raw, b_rows, x_in):
    heads, tokens = dt_raw.shape
    features = x_in.shape[1]
    width = features // heads
    per = min(4, heads)
    return pl.pallas_call(
        functools.partial(state_kernel, per),
        grid_spec=pltpu.PrefetchScalarGridSpec(
            num_scalar_prefetch=3,
            grid=(heads // per,),
            in_specs=[
                pl.BlockSpec((heads, tokens), lambda s, *_: (0, 0)),
                pl.BlockSpec(b_rows.shape, lambda s, *_: (0, 0)),
                pl.BlockSpec((tokens, per * width), lambda s, *_: (0, s)),
            ],
            out_specs=[
                pl.BlockSpec((LANES, per * width), lambda s, *_: (0, s)),
                pl.BlockSpec((8, per * width), lambda s, *_: (0, s)),
                pl.BlockSpec((tokens, LANES), lambda s, *_: (0, 0)),
            ],
            scratch_shapes=[
                pltpu.VMEM((LANES, tokens), F32),
                pltpu.VMEM((heads, tokens), F32),
                pltpu.VMEM((heads, LANES), F32),
            ],
        ),
        out_shape=[
            jax.ShapeDtypeStruct((LANES, features), BF16),
            jax.ShapeDtypeStruct((8, features), F32),
            jax.ShapeDtypeStruct((tokens, LANES), BF16),
        ],
        compiler_params=params(),
        name="block_states",
    )(meta, doc_lengths, a_log, dt_raw, b_rows, x_in)


def scan_kernel(meta, len_ref, alog_ref, skip_ref, dt_ref, b_ref, c_ref, x_ref, z_ref,
                part_ref, gate_ref, csel_ref, reach_ref, state_ref, past_ref, stack_ref):
    step = pl.program_id(0)
    heads = dt_ref.shape[0]
    groups = c_ref.shape[0] // LANES
    slot = max(8, heads)
    starts = starts_of(len_ref)
    block = meta[0]
    base = block + step * LANES

    @pl.when(step == 0)
    def _():
        state_ref[...] = jnp.zeros_like(state_ref)
        past_ref[...] = jnp.zeros_like(past_ref)
        stack_ref[...] = jnp.zeros_like(stack_ref)

    step_dt = softplus(dt_ref[...])
    decay = step_dt * rates(alog_ref, heads)
    total_to = running(decay, False)
    chunk_total = jnp.broadcast_to(total_to[:, LANES - 1:LANES], (heads, LANES))
    past = past_ref[...]
    before = total_to - jnp.log(step_dt) * LOG2E

    pos = base + lax.broadcasted_iota(I32, (heads, LANES), 1)
    doc = doc_at(pos, starts)
    doc_in = doc_at(base - 1, starts)
    doc_out = doc_at(base + LANES - 1, starts)
    doc_block = doc_at(block - 1, starts)
    into = jnp.where(doc == doc_in, jnp.exp2(total_to), 0.0)
    into_block = jnp.where(doc == doc_block, jnp.exp2(past + total_to), 0.0)
    fresh = jnp.where(doc == doc_out, jnp.exp2(chunk_total - total_to) * step_dt, 0.0)
    kept = jnp.exp2(chunk_total) * jnp.where(doc_in == doc_out, 1.0, 0.0)
    past_ref[...] = past + chunk_total

    stack_ref[0:heads, :] = total_to
    stack_ref[slot:slot + heads, :] = into
    stack_ref[2 * slot:2 * slot + heads, :] = into_block
    columns = stack_ref[...].T
    reach_ref[...] = columns

    row_pos = base + lax.broadcasted_iota(I32, (LANES, LANES), 0)
    col_pos = base + lax.broadcasted_iota(I32, (LANES, LANES), 1)
    keep = (row_pos >= col_pos) & (doc_at(row_pos, starts) == doc_at(col_pos, starts))
    chosen = dot(pick_matrix(meta[1], groups), c_ref[...])
    c_low = chosen.astype(BF16)
    csel_ref[...] = c_low
    b_low = b_ref[...]
    scores = lax.dot_general(c_low, b_low, (((1,), (1,)), ((), ())), preferred_element_type=F32)
    scores = jnp.where(keep, scores, 0.0)
    b_turned = b_low.astype(F32).T

    for h in range(heads):
        here = slice(h * LANES, (h + 1) * LANES)
        gaps = jnp.minimum(columns[:, h:h + 1] - before[h:h + 1, :], 80.0)
        weights = (jnp.exp2(gaps) * scores).astype(BF16)
        carried = (chosen * columns[:, slot + h:slot + h + 1]).astype(BF16)
        x_head = x_ref[:, here]
        state = state_ref[:, here]
        out = dot(jnp.concatenate([weights, carried], axis=1), jnp.concatenate([x_head, state.astype(BF16)], axis=0))
        out = out + skip_ref[h] * x_head.astype(F32)
        written = dot((b_turned * fresh[h:h + 1, :]).astype(BF16), x_head)
        state_ref[:, here] = state * kept[h:h + 1, :] + written
        z = z_ref[:, here].astype(F32)
        gate = z * (0.5 + 0.5 * jnp.tanh(0.5 * z))
        part_ref[:, here] = (out * gate).astype(BF16)
        gate_ref[:, here] = gate.astype(BF16)


def local_scan(meta, doc_lengths, a_log, d_skip, dt_raw, b_sel, c_rows, x_in, z_gate):
    heads, tokens = dt_raw.shape
    features = x_in.shape[1]
    chunks = tokens // LANES
    groups = c_rows.shape[0] // tokens
    wide = pl.BlockSpec((LANES, features), lambda s, *_: (s, 0))
    narrow = pl.BlockSpec((LANES, LANES), lambda s, *_: (s, 0))
    return pl.pallas_call(
        scan_kernel,
        grid_spec=pltpu.PrefetchScalarGridSpec(
            num_scalar_prefetch=4,
            grid=(chunks,),
            in_specs=[
                pl.BlockSpec((heads, LANES), lambda s, *_: (0, s)),
                narrow,
                pl.BlockSpec((LANES * groups, LANES), lambda s, *_: (s, 0)),
                wide,
                wide,
            ],
            out_specs=[wide, wide, narrow, narrow],
            scratch_shapes=[
                pltpu.VMEM((LANES, features), F32),
                pltpu.VMEM((heads, LANES), F32),
                pltpu.VMEM((LANES, LANES), F32),
            ],
        ),
        out_shape=[
            jax.ShapeDtypeStruct((tokens, features), BF16),
            jax.ShapeDtypeStruct((tokens, features), BF16),
            jax.ShapeDtypeStruct((tokens, LANES), BF16),
            jax.ShapeDtypeStruct((tokens, LANES), F32),
        ],
        compiler_params=params(),
        name="local_scan",
    )(meta, doc_lengths, a_log, d_skip, dt_raw, b_sel, c_rows, x_in, z_gate)


def tile_of(step, half, odd):
    return (step + (1 - odd) * half) % (2 * half)


def one_language(first, size, starts, lang_ref):
    lang = lang_at(first, starts, lang_ref)
    same = jnp.bool_(True)
    for d, s in enumerate(starts):
        inside = (s > first) & (s < first + size)
        same = same & jnp.logical_not(inside & (lang_ref[d] != lang))
    return lang, same


def has_language(which, first, size, starts, len_ref, lang_ref):
    found = jnp.bool_(False)
    for d, s in enumerate(starts):
        overlap = (s < first + size) & (s + len_ref[d] > first)
        found = found | (overlap & (lang_ref[d] == which))
    return found


def combine_kernel(n_states, slot, half, offset, meta, len_ref, lang_ref, c_ref, reach_ref, part_ref, gate_ref, gain_ref, down_ref, *rest):
    states, (gated_ref, other_ref, mine_ref, enter_ref, low_ref) = rest[:n_states], rest[n_states:]
    step = pl.program_id(0)
    tokens, features = part_ref.shape
    heads = features // LANES
    tile = tile_of(step, half, meta[2])
    first = meta[0] + (offset + tile) * tokens
    starts = starts_of(len_ref)

    if n_states > 1:
        @pl.when(step == 0)
        def _():
            total = states[0][...].astype(F32)
            for more in states[1:]:
                total = total + more[...].astype(F32)
            enter_ref[...] = total.astype(BF16)
        entering = enter_ref
    else:
        entering = states[0]

    squares = jnp.zeros((tokens, LANES), F32)
    c_low = c_ref[...]
    reach = reach_ref[...]
    pair = min(2, heads)
    for p in range(heads // pair):
        both = dot(c_low, entering[:, p * pair * LANES:(p + 1) * pair * LANES])
        for i in range(pair):
            h = p * pair + i
            here = slice(h * LANES, (h + 1) * LANES)
            entered = both[:, i * LANES:(i + 1) * LANES] * reach[:, 2 * slot + h:2 * slot + h + 1]
            gated = part_ref[:, here].astype(F32) + entered * gate_ref[:, here].astype(F32)
            squares = squares + gated * gated
            gated_ref[:, here] = (gated * gain_ref[:, here]).astype(BF16)

    lang, same = one_language(first, tokens, starts, lang_ref)

    @pl.when(same)
    def _():
        low_ref[...] = dot(gated_ref[...], down_ref[lang])

    @pl.when(jnp.logical_not(same))
    def _():
        low_ref[...] = jnp.zeros_like(low_ref)
        token_lang = lang_at(first + lax.broadcasted_iota(I32, (tokens, LANES), 0), starts, lang_ref)
        for k in range(down_ref.shape[0]):
            @pl.when(has_language(k, first, tokens, starts, len_ref, lang_ref))
            def _():
                low_ref[...] += jnp.where(token_lang == k, dot(gated_ref[...], down_ref[k]), 0.0)

    ones = jnp.ones((8, LANES), F32)
    sums = lax.dot_general(ones, squares, (((1,), (1,)), ((), ())), precision=lax.Precision.HIGHEST, preferred_element_type=F32)
    rows = jnp.concatenate([sums[:, :LANES], sums[:, LANES:]], axis=0)

    def message(ref):
        ref[0, 0:tokens, :] = low_ref[...].astype(BF16)
        ref[0, tokens:tokens + SUM_ROWS, :] = rows.astype(BF16)

    @pl.when(step < half)
    def _():
        message(other_ref)

    @pl.when(step >= half)
    def _():
        message(mine_ref)


TILE = 2 * LANES


def combine(meta, doc_lengths, doc_lang, c_sel, reach, part, gate, gain, down, states, offset, tiles, slot):
    features = part.shape[1]
    half = tiles // 2
    tile_map = lambda s, meta, *_: (offset + tile_of(s, half, meta[2]), 0)
    whole = lambda s, *_: (0, 0)
    return pl.pallas_call(
        functools.partial(combine_kernel, len(states), slot, half, offset),
        grid_spec=pltpu.PrefetchScalarGridSpec(
            num_scalar_prefetch=3,
            grid=(tiles,),
            in_specs=[
                pl.BlockSpec((TILE, LANES), tile_map),
                pl.BlockSpec((TILE, LANES), tile_map),
                pl.BlockSpec((TILE, features), tile_map),
                pl.BlockSpec((TILE, features), tile_map),
                pl.BlockSpec(gain.shape, whole),
                pl.BlockSpec(down.shape, lambda s, *_: (0, 0, 0)),
            ] + [pl.BlockSpec(v.shape, whole) for v in states],
            out_specs=[
                pl.BlockSpec((TILE, features), lambda s, meta, *_: (tile_of(s, half, meta[2]), 0)),
                pl.BlockSpec((1, TILE + SUM_ROWS, LANES), lambda s, *_: (jnp.minimum(s, half - 1), 0, 0)),
                pl.BlockSpec((1, TILE + SUM_ROWS, LANES), lambda s, *_: (jnp.maximum(s - half, 0), 0, 0)),
            ],
            scratch_shapes=[
                pltpu.VMEM(states[0].shape, BF16),
                pltpu.VMEM((TILE, LANES), F32),
            ],
        ),
        out_shape=[
            jax.ShapeDtypeStruct((tiles * TILE, features), BF16),
            jax.ShapeDtypeStruct((half, TILE + SUM_ROWS, LANES), BF16),
            jax.ShapeDtypeStruct((half, TILE + SUM_ROWS, LANES), BF16),
        ],
        compiler_params=params(),
        name="combine",
    )(meta, doc_lengths, doc_lang, c_sel, reach, part, gate, gain, down, *states)


def finish_kernel(half, offset, all_features, meta, len_ref, lang_ref, mine_ref, other_ref, gated_ref, up_ref, *rest):
    out_ref = rest[-1]
    step = pl.program_id(0)
    tokens, features = gated_ref.shape
    ranks = up_ref.shape[1]
    first = meta[0] + (offset + step) * tokens
    starts = starts_of(len_ref)
    is_mine = (step // half) == meta[2]
    message = jnp.where(is_mine, mine_ref[0].astype(F32), other_ref[0].astype(F32))
    scale = lax.rsqrt(message[tokens:tokens + SUM_ROWS, :] / all_features + EPS)
    turned = jnp.concatenate([scale] * (LANES // SUM_ROWS), axis=0).T
    scale = jnp.concatenate([turned[:, 0:1], turned[:, 8:9]], axis=0)
    low = (message[0:tokens, :] * scale).astype(BF16)
    lang, same = one_language(first, tokens, starts, lang_ref)
    piece = min(4 * LANES, features)

    @pl.when(same)
    def _():
        for at in range(0, features, piece):
            here = slice(at, at + piece)
            lifted = dot(low, up_ref[lang, :, here])
            out_ref[:, here] = (gated_ref[:, here].astype(F32) * scale + lifted).astype(BF16)

    @pl.when(jnp.logical_not(same))
    def _():
        token_lang = lang_at(first + lax.broadcasted_iota(I32, (tokens, LANES), 0), starts, lang_ref)
        zero = jnp.zeros((), BF16)
        spread = jnp.concatenate([jnp.where(token_lang == k, low, zero) for k in range(up_ref.shape[0])], axis=1)
        for at in range(0, features, piece):
            here = slice(at, at + piece)
            lifted = dot(spread, up_ref[:, :, here].reshape(up_ref.shape[0] * ranks, piece))
            out_ref[:, here] = (gated_ref[:, here].astype(F32) * scale + lifted).astype(BF16)


def finish(meta, doc_lengths, doc_lang, mine, other, gated, up, offset, all_tiles, all_features, into=None):
    features = gated.shape[1]
    tiles = gated.shape[0] // TILE
    half = tiles // 2
    part = pl.BlockSpec((1, TILE + SUM_ROWS, LANES), lambda s, *_: (s % half, 0, 0))
    more = [] if into is None else [into]
    return pl.pallas_call(
        functools.partial(finish_kernel, half, offset, all_features),
        grid_spec=pltpu.PrefetchScalarGridSpec(
            num_scalar_prefetch=3,
            grid=(tiles,),
            in_specs=[
                part,
                part,
                pl.BlockSpec((TILE, features), lambda s, *_: (s, 0)),
                pl.BlockSpec(up.shape, lambda s, *_: (0, 0, 0)),
            ] + [pl.BlockSpec(memory_space=pl.ANY) for _ in more],
            out_specs=pl.BlockSpec((TILE, features), lambda s, *_: (offset + s, 0)),
        ),
        out_shape=jax.ShapeDtypeStruct((all_tiles * TILE, features), BF16),
        input_output_aliases={7: 0} if more else {},
        compiler_params=params(),
        name="finish",
    )(meta, doc_lengths, doc_lang, mine, other, gated, up, *more)


def sum_over_head(other, mine, devices):
    def across(v, mask):
        return lax.ppermute(v, "head", [(i, i ^ mask) for i in range(devices)])

    if devices == 1:
        return mine, other
    total = (mine.astype(F32) + across(other, 1).astype(F32)).astype(BF16)
    bit = 2
    while bit < devices:
        masks = [bit] if 2 * bit >= devices else [bit, 2 * bit, 3 * bit]
        arrived = [across(total, m) for m in masks]
        added = total.astype(F32)
        for a in arrived:
            added = added + a.astype(F32)
        total = added.astype(BF16)
        bit *= 2 ** (1 if len(masks) == 1 else 2)
    return total, across(total, 1)


def per_device(seq_size, head_size, x_in, z_gate, b_input, c_input, dt_raw, a_log, d_skip, norm_gain,
               doc_lengths, doc_lang, adapt_down, adapt_up):
    tokens, features = x_in.shape
    heads = dt_raw.shape[0]
    groups = b_input.shape[1]
    head_rank = lax.axis_index("head")
    group = head_rank * heads // (heads * head_size // groups)
    meta = jnp.stack([lax.axis_index("seq") * tokens, group, head_rank % 2]).astype(I32)
    b_rows = b_input.reshape(tokens * groups, b_input.shape[2])
    c_rows = c_input.reshape(tokens * groups, c_input.shape[2])
    longest = tokens * seq_size // LONGEST_SHARE
    hops = min(-(-(longest - 1) // tokens), seq_size - 1)

    state, through, b_sel = block_states(meta, doc_lengths, a_log, dt_raw, b_rows, x_in)
    onward = [(i, i + 1) for i in range(seq_size - 1)]
    states = []
    for hop in range(hops):
        if hop > 0:
            state = (state.astype(F32) * through[0:1]).astype(BF16)
        state = lax.ppermute(state, "seq", onward)
        states.append(state)
    part, gate, c_sel, reach = local_scan(meta, doc_lengths, a_log, d_skip, dt_raw, b_sel, c_rows, x_in, z_gate)
    slot = max(8, heads)
    all_tiles = tokens // TILE
    gated, other, mine = combine(
        meta, doc_lengths, doc_lang, c_sel, reach, part, gate, norm_gain.reshape(1, features), adapt_down, states, 0, all_tiles, slot
    )
    mine, other = sum_over_head(other, mine, head_size)
    return finish(meta, doc_lengths, doc_lang, mine, other, gated, adapt_up, 0, all_tiles, features * head_size)


def solution(mesh):
    placed = (
        P("seq", "head"),
        P("seq", "head"),
        P("seq", None, None),
        P("seq", None, None),
        P("head", "seq"),
        P("head"),
        P("head"),
        P("head"),
        P(),
        P(),
        P(None, "head", None),
        P(None, None, "head"),
    )
    return jax.shard_map(
        functools.partial(per_device, mesh.shape["seq"], mesh.shape["head"]),
        mesh=mesh, in_specs=placed, out_specs=P("seq", "head"), check_vma=False,
    )
```

time: 347 us -> 78.9 us (0.23)
  matrix products: 98.2 us -> 0 us
  local copies, waits for them, and re-layouts: 77.5 us -> 3.78 us
  blocking collectives: 57.2 us -> 0 us
  other arithmetic: 54.2 us -> 0.3 us
  Pallas kernels: 0 us -> 40.1 us
  waiting for transfers between devices: 41.8 us -> 20 us
  between operations: 14.2 us -> 0.13 us
  starting transfers between devices: 0.01 us -> 13 us
    dot_general x35 -> x0, matrix products: 98.2 us -> none  [the longest x8 27.2 us: advance(): inner_part = jnp.einsum('hij,hjp->hip', weights, x_float, precision=highest)]
    psum x2 -> x0, blocking collectives: 43.3 us -> none  [the longest x1 29.7 us: per_device(): low_rank = lax.psum(picked, 'head').astype(jnp.bfloat16)]
    all_gather x1 -> x0, waiting for transfers between devices: 41.8 us -> none  [per_device(): shards = lax.all_gather(local_state[None], 'seq', axis=0, tiled=True)]
    pallas_call x0 -> x4, Pallas kernels: none -> 40.1 us  [the longest x1 18.4 us: local_scan(): pl.pallas_call(scan_kernel, grid_spec=pltpu.PrefetchScalarGridSpec(num_sc...]
    reshape x3 -> x0, local copies, waits for them, and re-layouts: 24 us -> none  [the longest x1 9.54 us: block_scan(): outputs.transpose(1, 0, 2, 3).reshape(head_count, length, head_width)]
    ppermute x0 -> x7, waiting for transfers between devices: none -> 20 us  [the longest x2 11.1 us: per_device(): state = lax.ppermute(state, 'seq', onward)]
    mul x18 -> x0, other arithmetic: 17.4 us -> none  [the longest x8 10.4 us: advance(): kept_share = jnp.exp(cumulative[:, -1]) * reach_mask[-1]]
    slice x27 -> x1, local copies, waits for them, and re-layouts: 16.2 us -> 0.01 us  [per_device(): state = (state.astype(F32) * through[0:1]).astype(BF16)]
  transfers between devices with their start and end apart: 1 -> 7, of which waited for: 1 -> 6; matrix products, arithmetic and copies ran while one was open for 8% -> 0% of each run, Pallas kernels for 0% -> 24%
where the time goes in v1:
time: 78.9 us; the launch traced here: 77.4 us
  Pallas kernels  40.1 us (51%)
  waiting for transfers between devices  20 us (25%)
  starting transfers between devices  13 us (16%)
  local copies, waits for them, and re-layouts  3.78 us (5%)
    pallas_call x1, Pallas kernels, local_scan(): pl.pallas_call(scan_kernel, grid_spec=pltpu.PrefetchScalarGridSpec(num_sc...  18.4 us
    ppermute x2, waiting for transfers between devices, per_device(): state = lax.ppermute(state, 'seq', onward)  11.1 us
    pallas_call x1, Pallas kernels, combine(): pl.pallas_call(functools.partial(combine_kernel, len(states), slot, half,...  9.89 us
    ppermute x2, starting transfers between devices, per_device(): state = lax.ppermute(state, 'seq', onward)  9.39 us
    ppermute x5, waiting for transfers between devices, across(): return lax.ppermute(v, 'head', [(i, i ^ mask) for i in range(devices)])  8.92 us
    pallas_call x1, Pallas kernels, finish(): pl.pallas_call(functools.partial(finish_kernel, half, offset, all_feature...  6.52 us
    pallas_call x1, Pallas kernels, block_states(): pl.pallas_call(functools.partial(state_kernel, per), grid_spec=pltpu.Pref...  5.35 us
    unnamed x20, local copies, waits for them, and re-layouts  3.77 us
  transfers between devices with their start and end apart: 7, of which 6 were waited for; matrix products, arithmetic and copies ran while one was open for 0% of the time, Pallas kernels for 24%

profile of v1, /device:TPU:0, one launch (start us, length us, event | category | flops | bytes accessed | tf_op | source)
XLA Modules:
  0.0 77.4 jit_solution(2359011614973833816)
XLA Ops:
  0.0 0.1 pad_add_fusion.meta
  0.1 1.6 %copy-done = bf16[1024,8,128]{2,1,0:T(8,128)(2,1)S(1)} copy-done((bf16[1024,8,128]{2,1,0:T(8,128)(2,1)S(1)}, bf16[1024,8,128]{2,1,0:T(8,128)(2,1)}, u32[]{:S(2)}) %copy-start) | copy-done | bytes 2097176
  1.7 0.8 %copy-done.4 = f32[16,1024]{1,0:T(8,128)S(1)} copy-done((f32[16,1024]{1,0:T(8,128)S(1)}, f32[16,1024]{1,0:T(8,128)}, u32[]{:S(2)}) %copy-start.4) | copy-done | bytes 65560
  2.5 0.7 copy-done.5
  3.2 0.7 copy-done.7
  3.8 5.3 %block_states.1 = (bf16[128,2048]{1,0:T(8,128)(2,1)S(1)}, f32[8,2048]{1,0:T(8,128)S(1)}, bf16[1024,128]{1,0:T(8,128)(2,1)S(1)}) custom-call(s32[3]{0:T(128)S(1)} %pad_add_fusion.meta, s32[6]{0:T(128)S(1)} %copy-done.5, f32[16]{0:T(128)S(1)} %copy-done.7, f32[16,1024]{1,0:T(8,128)S(1)} %copy-done.4, bf16[8192,128]{1,0:T(8,128)(2,1)S(1)} %bitcast.7, ...), custom_call_target="tpu_custom_call" | custom-call | tf_op jit(solution)/shard_map/block_states/pallas_call | solution.py:131
  9.2 5.0 %collective-permute-start = (bf16[128,2048]{1,0:T(8,128)(2,1)S(1)}, bf16[128,2048]{1,0:T(8,128)(2,1)S(1)}, u32[]{:S(2)}, u32[]{:S(2)}) collective-permute-start(bf16[128,2048]{1,0:T(8,128)(2,1)S(1)} %get-tuple-element.20), channel_id=1, source_target_pairs={{0,8},{8,16},{16,24},{1,9},{9,17},{17,25},{2,10},{10,18},{18,26},{... | collective-permute-start | bytes 1572872 | tf_op jit(solution)/shard_map/ppermute | solution.py:493
  14.2 11.1 %collective-permute-done.rest_0_ = bf16[128,2048]{1,0:T(8,128)(2,1)S(1)} collective-permute-done((bf16[128,2048]{1,0:T(8,128)(2,1)S(1)}, bf16[128,2048]{1,0:T(8,128)(2,1)S(1)}, u32[]{:S(2)}, u32[]{:S(2)}) %collective-permute-start) | collective-permute-done | bytes 524320 | tf_op jit(solution)/shard_map/ppermute | solution.py:493
  25.3 0.1 multiply_convert_fusion
  25.4 4.4 %collective-permute-start.1 = (bf16[128,2048]{1,0:T(8,128)(2,1)S(1)}, bf16[128,2048]{1,0:T(8,128)(2,1)S(1)}, u32[]{:S(2)}, u32[]{:S(2)}) collective-permute-start(bf16[128,2048]{1,0:T(8,128)(2,1)S(1)} %multiply_convert_fusion), channel_id=1, source_target_pairs={{0,8},{8,16},{16,24},{1,9},{9,17},{17,25},{2,10},{10,18},{18,26},{... | collective-permute-start | bytes 1572872 | tf_op jit(solution)/shard_map/ppermute | solution.py:493
  29.8 0.0 copy-done.9
  29.8 0.0 copy-done.1
  29.8 0.0 copy-start.2
  29.9 0.0 copy-start.6
  29.9 0.0 copy-start.8
  29.9 18.4 %local_scan.1 = (bf16[1024,2048]{1,0:T(8,128)(2,1)}, bf16[1024,2048]{1,0:T(8,128)(2,1)}, bf16[1024,128]{1,0:T(8,128)(2,1)S(1)}, f32[1024,128]{1,0:T(8,128)S(1)}) custom-call(s32[3]{0:T(128)S(1)} %pad_add_fusion.meta, s32[6]{0:T(128)S(1)} %copy-done.5, f32[16]{0:T(128)S(1)} %copy-done.7, f32[16]{0:T(128)S(1)} %copy-done.9, f32[16,1024]{1,0:T(8,128)S(1)} %copy-done.4, ...), custom_call_target="tpu_custom_call" | custom-call | tf_op jit(solution)/shard_map/local_scan/pallas_call | solution.py:237
  48.3 0.0 collective-permute-done.1.rest_1_
  48.3 0.0 copy-done.2
  48.3 0.0 copy-start.3
  48.3 9.9 %combine.1 = (bf16[1024,2048]{1,0:T(8,128)(2,1)}, bf16[2,272,128]{2,1,0:T(8,128)(2,1)S(1)}, bf16[2,272,128]{2,1,0:T(8,128)(2,1)S(1)}) custom-call(s32[3]{0:T(128)S(1)} %pad_add_fusion.meta, s32[6]{0:T(128)S(1)} %copy-done.5, s32[6]{0:T(128)S(1)} %copy-done.8, bf16[1024,128]{1,0:T(8,128)(2,1)S(1)} %get-tuple-element.16.c_ref, ...), custom_call_target="tpu_custom_call" | custom-call | tf_op jit(solution)/shard_map/combine/pallas_call | solution.py:362
  58.2 0.0 collective-permute-start.2
  58.2 1.4 %collective-permute-done.2 = bf16[2,272,128]{2,1,0:T(8,128)(2,1)S(1)} collective-permute-done((bf16[2,272,128]{2,1,0:T(8,128)(2,1)S(1)}, bf16[2,272,128]{2,1,0:T(8,128)(2,1)S(1)}, u32[]{:S(2)}, u32[]{:S(2)}) %collective-permute-start.2) | collective-permute-done | bytes 139296 | tf_op jit(solution)/shard_map/ppermute | solution.py:457
  59.6 2.5 %collective-permute-start.5 = (bf16[2,272,128]{2,1,0:T(8,128)(2,1)S(1)}, bf16[2,272,128]{2,1,0:T(8,128)(2,1)S(1)}, u32[]{:S(2)}, u32[]{:S(2)}) collective-permute-start(bf16[2,272,128]{2,1,0:T(8,128)(2,1)S(1)} %add_convert_fusion.1), channel_id=1, source_target_pairs={{0,6},{1,7},{2,4},{3,5},{4,2},{5,3},{6,0},{7,1},{8,14},{9,15},{10,... | collective-permute-start | bytes 417800 | tf_op jit(solution)/shard_map/ppermute | solution.py:457
  62.1 0.5 collective-permute-start.4
  62.6 0.5 collective-permute-start.3
  63.1 3.6 %collective-permute-done.5 = bf16[2,272,128]{2,1,0:T(8,128)(2,1)S(1)} collective-permute-done((bf16[2,272,128]{2,1,0:T(8,128)(2,1)S(1)}, bf16[2,272,128]{2,1,0:T(8,128)(2,1)S(1)}, u32[]{:S(2)}, u32[]{:S(2)}) %collective-permute-start.5) | collective-permute-done | bytes 139296 | tf_op jit(solution)/shard_map/ppermute | solution.py:457
  66.8 2.5 %collective-permute-done.4 = bf16[2,272,128]{2,1,0:T(8,128)(2,1)S(1)} collective-permute-done((bf16[2,272,128]{2,1,0:T(8,128)(2,1)S(1)}, bf16[2,272,128]{2,1,0:T(8,128)(2,1)S(1)}, u32[]{:S(2)}, u32[]{:S(2)}) %collective-permute-start.4) | collective-permute-done | bytes 139296 | tf_op jit(solution)/shard_map/ppermute | solution.py:457
  69.3 0.1 collective-permute-done.3
  69.4 0.1 add_convert_fusion.mine_ref
  69.5 0.1 collective-permute-start.6
  69.5 1.3 %collective-permute-done.6.other_ref = bf16[2,272,128]{2,1,0:T(8,128)(2,1)S(1)} collective-permute-done((bf16[2,272,128]{2,1,0:T(8,128)(2,1)S(1)}, bf16[2,272,128]{2,1,0:T(8,128)(2,1)S(1)}, u32[]{:S(2)}, u32[]{:S(2)}) %collective-permute-start.6) | collective-permute-done | bytes 139296 | tf_op jit(solution)/shard_map/ppermute | solution.py:457
  70.9 6.5 %finish.1 = bf16[1024,2048]{1,0:T(8,128)(2,1)} custom-call(s32[3]{0:T(128)S(1)} %pad_add_fusion.meta, s32[6]{0:T(128)S(1)} %copy-done.5, s32[6]{0:T(128)S(1)} %copy-done.8, bf16[2,272,128]{2,1,0:T(8,128)(2,1)S(1)} %add_convert_fusion.mine_ref, bf16[2,272,128]{2,1,0:T(8,128)(2,1)S(1)} %collective-permute-done.6.other_ref, ...), custom_call_target="tpu_custom_call" | custom-call | tf_op jit(solution)/shard_map/finish/pallas_call | solution.py:435
  (11 shorter events, 0.1 us)
Async XLA Ops:
  0.0 29.8 %copy-start.9 = (f32[16]{0:T(128)S(1)}, f32[16]{0:T(128)}, u32[]{:S(2)}) copy-start(f32[16]{0:T(128)} %skip_ref.1) | copy-start | bytes 196
  0.1 1.6 %copy-start = (bf16[1024,8,128]{2,1,0:T(8,128)(2,1)S(1)}, bf16[1024,8,128]{2,1,0:T(8,128)(2,1)}, u32[]{:S(2)}) copy-start(bf16[1024,8,128]{2,1,0:T(8,128)(2,1)} %param.14) | copy-start | bytes 6291460
  1.7 0.8 %copy-start.4 = (f32[16,1024]{1,0:T(8,128)S(1)}, f32[16,1024]{1,0:T(8,128)}, u32[]{:S(2)}) copy-start(f32[16,1024]{1,0:T(8,128)} %dt_ref.3) | copy-start | bytes 196612
  2.5 0.7 copy-start.5
  3.2 0.7 copy-start.7
  3.8 26.0 %copy-start.1 = (bf16[1024,8,128]{2,1,0:T(8,128)(2,1)S(1)}, bf16[1024,8,128]{2,1,0:T(8,128)(2,1)}, u32[]{:S(2)}) copy-start(bf16[1024,8,128]{2,1,0:T(8,128)(2,1)} %param.15) | copy-start | bytes 6291460
  9.2 16.1 %collective-permute-start = (bf16[128,2048]{1,0:T(8,128)(2,1)S(1)}, bf16[128,2048]{1,0:T(8,128)(2,1)S(1)}, u32[]{:S(2)}, u32[]{:S(2)}) collective-permute-start(bf16[128,2048]{1,0:T(8,128)(2,1)S(1)} %get-tuple-element.20), channel_id=1, source_target_pairs={{0,8},{8,16},{16,24},{1,9},{9,17},{17,25},{2,10},{10,18},{18,26},{... | collective-permute-start | bytes 1572872 | tf_op jit(solution)/shard_map/ppermute | solution.py:493
  25.4 22.9 %collective-permute-start.1 = (bf16[128,2048]{1,0:T(8,128)(2,1)S(1)}, bf16[128,2048]{1,0:T(8,128)(2,1)S(1)}, u32[]{:S(2)}, u32[]{:S(2)}) collective-permute-start(bf16[128,2048]{1,0:T(8,128)(2,1)S(1)} %multiply_convert_fusion), channel_id=1, source_target_pairs={{0,8},{8,16},{16,24},{1,9},{9,17},{17,25},{2,10},{10,18},{18,26},{... | collective-permute-start | bytes 1572872 | tf_op jit(solution)/shard_map/ppermute | solution.py:493
  29.8 18.4 %copy-start.2 = (bf16[4,2048,128]{2,1,0:T(8,128)(2,1)S(1)}, bf16[4,2048,128]{2,1,0:T(8,128)(2,1)}, u32[]{:S(2)}) copy-start(bf16[4,2048,128]{2,1,0:T(8,128)(2,1)} %down_ref.1) | copy-start | bytes 6291460
  29.9 18.4 %copy-start.6 = (f32[2048]{0:T(1024)S(1)}, f32[2048]{0:T(1024)}, u32[]{:S(2)}) copy-start(f32[2048]{0:T(1024)} %param.19) | copy-start | bytes 24580
  29.9 18.4 %copy-start.8 = (s32[6]{0:T(128)S(1)}, s32[6]{0:T(128)}, u32[]{:S(2)}) copy-start(s32[6]{0:T(128)} %lang_ref.3) | copy-start | bytes 76
  48.3 22.6 %copy-start.3 = (bf16[4,128,2048]{2,1,0:T(8,128)(2,1)S(1)}, bf16[4,128,2048]{2,1,0:T(8,128)(2,1)}, u32[]{:S(2)}) copy-start(bf16[4,128,2048]{2,1,0:T(8,128)(2,1)} %up_ref.1) | copy-start | bytes 6291460
  58.2 1.4 %collective-permute-start.2 = (bf16[2,272,128]{2,1,0:T(8,128)(2,1)S(1)}, bf16[2,272,128]{2,1,0:T(8,128)(2,1)S(1)}, u32[]{:S(2)}, u32[]{:S(2)}) collective-permute-start(bf16[2,272,128]{2,1,0:T(8,128)(2,1)S(1)} %get-tuple-element.23), channel_id=1, source_target_pairs={{0,1},{1,0},{2,3},{3,2},{4,5},{5,4},{6,7},{7,6},{8,9},{9,8},{10,11... | collective-permute-start | bytes 417800 | tf_op jit(solution)/shard_map/ppermute | solution.py:457
  59.6 7.2 %collective-permute-start.5 = (bf16[2,272,128]{2,1,0:T(8,128)(2,1)S(1)}, bf16[2,272,128]{2,1,0:T(8,128)(2,1)S(1)}, u32[]{:S(2)}, u32[]{:S(2)}) collective-permute-start(bf16[2,272,128]{2,1,0:T(8,128)(2,1)S(1)} %add_convert_fusion.1), channel_id=1, source_target_pairs={{0,6},{1,7},{2,4},{3,5},{4,2},{5,3},{6,0},{7,1},{8,14},{9,15},{10,... | collective-permute-start | bytes 417800 | tf_op jit(solution)/shard_map/ppermute | solution.py:457
  62.1 7.2 %collective-permute-start.4 = (bf16[2,272,128]{2,1,0:T(8,128)(2,1)S(1)}, bf16[2,272,128]{2,1,0:T(8,128)(2,1)S(1)}, u32[]{:S(2)}, u32[]{:S(2)}) collective-permute-start(bf16[2,272,128]{2,1,0:T(8,128)(2,1)S(1)} %add_convert_fusion.1), channel_id=1, source_target_pairs={{0,4},{1,5},{2,6},{3,7},{4,0},{5,1},{6,2},{7,3},{8,12},{9,13},{10,... | collective-permute-start | bytes 417800 | tf_op jit(solution)/shard_map/ppermute | solution.py:457
  62.6 6.8 %collective-permute-start.3 = (bf16[2,272,128]{2,1,0:T(8,128)(2,1)S(1)}, bf16[2,272,128]{2,1,0:T(8,128)(2,1)S(1)}, u32[]{:S(2)}, u32[]{:S(2)}) collective-permute-start(bf16[2,272,128]{2,1,0:T(8,128)(2,1)S(1)} %add_convert_fusion.1), channel_id=1, source_target_pairs={{0,2},{1,3},{2,0},{3,1},{4,6},{5,7},{6,4},{7,5},{8,10},{9,11},{10,... | collective-permute-start | bytes 417800 | tf_op jit(solution)/shard_map/ppermute | solution.py:457
  69.5 1.4 %collective-permute-start.6 = (bf16[2,272,128]{2,1,0:T(8,128)(2,1)S(1)}, bf16[2,272,128]{2,1,0:T(8,128)(2,1)S(1)}, u32[]{:S(2)}, u32[]{:S(2)}) collective-permute-start(bf16[2,272,128]{2,1,0:T(8,128)(2,1)S(1)} %add_convert_fusion.mine_ref), channel_id=1, source_target_pairs={{0,1},{1,0},{2,3},{3,2},{4,5},{5,4},{6,7},{7,6},{8,9},{9,8},{10,11... | collective-permute-start | bytes 417800 | tf_op jit(solution)/shard_map/ppermute | solution.py:457

commit v2 on v1

v2 whole, which is shorter than its diff:
```python
import functools

import jax
import jax.numpy as jnp
from jax import lax
from jax.experimental import pallas as pl
from jax.experimental.pallas import tpu as pltpu
from jax.sharding import PartitionSpec as P

F32 = jnp.float32
BF16 = jnp.bfloat16
I32 = jnp.int32
LOG2E = 1.4426950408889634
EPS = 1e-05
LANES = 128
SUM_ROWS = 16
LONGEST_SHARE = 3
VMEM_LIMIT = 16 * 1024 * 1024


def params():
    return pltpu.CompilerParams(vmem_limit_bytes=VMEM_LIMIT)


def starts_of(docs):
    starts, at = [], jnp.int32(0)
    for d in range(docs.shape[0] // 2):
        starts.append(at)
        at = at + docs[d]
    return starts


def langs_of(docs):
    count = docs.shape[0] // 2
    return [docs[count + d] for d in range(count)]


def doc_at(pos, starts):
    found = jnp.where(pos >= starts[0], 0, -1)
    for s in starts[1:]:
        found = found + jnp.where(pos >= s, 1, 0)
    return found


def lang_at(pos, starts, lang_ref):
    found = jnp.where(pos >= 0, lang_ref[0], 0)
    for d in range(1, len(starts)):
        found = jnp.where(pos >= starts[d], lang_ref[d], found)
    return found


def rates(alog_ref, rows):
    which = lax.broadcasted_iota(I32, (rows, LANES), 0)
    column = jnp.zeros((rows, LANES), F32)
    for h in range(rows):
        column = jnp.where(which == h, alog_ref[h], column)
    return -LOG2E * jnp.exp(column)


def softplus(v):
    return jnp.maximum(v, 0.0) + jnp.log(1.0 + jnp.exp(-jnp.abs(v)))


def running(v, back):
    width = v.shape[1]
    lane = lax.broadcasted_iota(I32, v.shape, 1)
    step = 1
    while step < width:
        if back:
            v = v + jnp.where(lane + step < width, pltpu.roll(v, width - step, 1), 0.0)
        else:
            v = v + jnp.where(lane >= step, pltpu.roll(v, step, 1), 0.0)
        step *= 2
    return v


def pick_matrix(group, groups):
    shape = (LANES, LANES * groups)
    row = lax.broadcasted_iota(I32, shape, 0)
    col = lax.broadcasted_iota(I32, shape, 1)
    return jnp.where(col == row * groups + group, 1.0, 0.0).astype(BF16)


def dot(a, b):
    return jnp.dot(a, b, preferred_element_type=F32)


def state_kernel(x_parts, b_parts, meta, docs, alog_ref, dt_hbm, b_hbm, x_hbm, state_ref, thr_ref, bsel_ref, x_ref,
                 dt_ref, b_ref, bt_ref, w_ref, all_ref, sems):
    heads, tokens = dt_ref.shape
    groups = b_ref.shape[0] // tokens
    features = x_ref.shape[1]
    rows = b_ref.shape[0] // b_parts
    wide = features // x_parts
    dt_copy = pltpu.make_async_copy(dt_hbm, dt_ref, sems.at[0])
    b_copies = [
        pltpu.make_async_copy(b_hbm.at[pl.ds(i * rows, rows)], b_ref.at[pl.ds(i * rows, rows)], sems.at[1 + i])
        for i in range(b_parts)
    ]
    x_copies = [
        pltpu.make_async_copy(x_hbm.at[:, pl.ds(i * wide, wide)], x_ref.at[:, pl.ds(i * wide, wide)], sems.at[1 + b_parts + i])
        for i in range(x_parts)
    ]
    for copy in [dt_copy] + b_copies + x_copies:
        copy.start()

    dt_copy.wait()
    starts = starts_of(docs)
    base = meta[0]
    rate = rates(alog_ref, heads)
    parts, totals = [], []
    for c in range(tokens // LANES):
        step_dt = softplus(dt_ref[:, c * LANES:(c + 1) * LANES])
        decay = step_dt * rate
        after = running(decay, True)
        parts.append((step_dt, after - decay))
        totals.append(after[:, 0:1])
    last_doc = doc_at(base + tokens - 1, starts)
    first_doc = doc_at(base - 1, starts)
    later = jnp.zeros((heads, 1), F32)
    for c in reversed(range(tokens // LANES)):
        step_dt, inside = parts[c]
        pos = base + c * LANES + lax.broadcasted_iota(I32, (heads, LANES), 1)
        alive = doc_at(pos, starts) == last_doc
        w_ref[:, c * LANES:(c + 1) * LANES] = jnp.where(alive, jnp.exp2(inside + later) * step_dt, 0.0)
        later = later + totals[c]
    kept = jnp.where(last_doc == first_doc, 1.0, 0.0)
    all_ref[...] = jnp.broadcast_to(jnp.exp2(later) * kept, all_ref.shape)

    pick = pick_matrix(meta[1], groups)
    per = tokens // LANES // b_parts
    for i in range(b_parts):
        b_copies[i].wait()
        for c in range(i * per, (i + 1) * per):
            here = slice(c * LANES, (c + 1) * LANES)
            chosen = dot(pick, b_ref[c * LANES * groups:(c + 1) * LANES * groups, :])
            bsel_ref[here, :] = chosen.astype(BF16)
            bt_ref[:, here] = chosen.T

    for i in range(x_parts):
        x_copies[i].wait()
        for h in range(i * heads // x_parts, (i + 1) * heads // x_parts):
            here = slice(h * LANES, (h + 1) * LANES)
            weighted = (bt_ref[...] * w_ref[h:h + 1, :]).astype(BF16)
            state_ref[:, here] = dot(weighted, x_ref[:, here]).astype(BF16)
            thr_ref[:, here] = jnp.broadcast_to(all_ref[h:h + 1, :], (8, LANES))


def in_vmem():
    return pl.BlockSpec(memory_space=pltpu.VMEM)


def block_states(meta, docs, a_log, dt_raw, b_rows, x_in):
    heads, tokens = dt_raw.shape
    features = x_in.shape[1]
    x_parts, b_parts = min(4, heads), 4
    anywhere = pl.BlockSpec(memory_space=pl.ANY)
    return pl.pallas_call(
        functools.partial(state_kernel, x_parts, b_parts),
        grid_spec=pltpu.PrefetchScalarGridSpec(
            num_scalar_prefetch=3,
            grid=(1,),
            in_specs=[anywhere, anywhere, anywhere],
            out_specs=[in_vmem(), in_vmem(), in_vmem(), in_vmem()],
            scratch_shapes=[
                pltpu.VMEM((heads, tokens), F32),
                pltpu.VMEM(b_rows.shape, BF16),
                pltpu.VMEM((LANES, tokens), F32),
                pltpu.VMEM((heads, tokens), F32),
                pltpu.VMEM((heads, LANES), F32),
                pltpu.SemaphoreType.DMA((1 + b_parts + x_parts,)),
            ],
        ),
        out_shape=[
            pltpu.VMEM((LANES, features), BF16),
            pltpu.VMEM((8, features), F32),
            pltpu.VMEM((tokens, LANES), BF16),
            pltpu.VMEM((tokens, features), BF16),
        ],
        compiler_params=params(),
        cost_estimate=pl.CostEstimate(flops=2 * LANES * tokens * features, bytes_accessed=8 * tokens * features, transcendentals=0),
        name="block_states",
    )(meta, docs, a_log, *[pltpu.with_memory_space_constraint(v, pltpu.HBM) for v in (dt_raw, b_rows, x_in)])


def scan_kernel(meta, docs, alog_ref, skip_ref, dt_ref, b_ref, c_ref, x_ref, z_ref,
                part_ref, gate_ref, csel_ref, reach_ref, state_ref, past_ref, stack_ref):
    step = pl.program_id(0)
    heads, tokens = dt_ref.shape
    groups = c_ref.shape[0] // tokens
    slot = max(8, heads)
    starts = starts_of(docs)
    now = pl.ds(pl.multiple_of(step * LANES, LANES), LANES)
    block = meta[0]
    base = block + step * LANES

    @pl.when(step == 0)
    def _():
        state_ref[...] = jnp.zeros_like(state_ref)
        past_ref[...] = jnp.zeros_like(past_ref)
        stack_ref[...] = jnp.zeros_like(stack_ref)

    step_dt = softplus(dt_ref[:, now])
    decay = step_dt * rates(alog_ref, heads)
    total_to = running(decay, False)
    chunk_total = jnp.broadcast_to(total_to[:, LANES - 1:LANES], (heads, LANES))
    past = past_ref[...]
    before = total_to - jnp.log(step_dt) * LOG2E

    pos = base + lax.broadcasted_iota(I32, (heads, LANES), 1)
    doc = doc_at(pos, starts)
    doc_in = doc_at(base - 1, starts)
    doc_out = doc_at(base + LANES - 1, starts)
    doc_block = doc_at(block - 1, starts)
    into = jnp.where(doc == doc_in, jnp.exp2(total_to), 0.0)
    into_block = jnp.where(doc == doc_block, jnp.exp2(past + total_to), 0.0)
    fresh = jnp.where(doc == doc_out, jnp.exp2(chunk_total - total_to) * step_dt, 0.0)
    kept = jnp.exp2(chunk_total) * jnp.where(doc_in == doc_out, 1.0, 0.0)
    past_ref[...] = past + chunk_total

    stack_ref[0:heads, :] = total_to
    stack_ref[slot:slot + heads, :] = into
    stack_ref[2 * slot:2 * slot + heads, :] = into_block
    columns = stack_ref[...].T
    reach_ref[now, :] = columns

    row_pos = base + lax.broadcasted_iota(I32, (LANES, LANES), 0)
    col_pos = base + lax.broadcasted_iota(I32, (LANES, LANES), 1)
    keep = (row_pos >= col_pos) & (doc_at(row_pos, starts) == doc_at(col_pos, starts))
    chosen = dot(pick_matrix(meta[1], groups), c_ref[pl.ds(pl.multiple_of(step * LANES * groups, LANES), LANES * groups), :])
    c_low = chosen.astype(BF16)
    csel_ref[now, :] = c_low
    b_low = b_ref[now, :]
    scores = lax.dot_general(c_low, b_low, (((1,), (1,)), ((), ())), preferred_element_type=F32)
    scores = jnp.where(keep, scores, 0.0)
    b_turned = b_low.astype(F32).T

    for h in range(heads):
        here = slice(h * LANES, (h + 1) * LANES)
        gaps = jnp.minimum(columns[:, h:h + 1] - before[h:h + 1, :], 80.0)
        weights = (jnp.exp2(gaps) * scores).astype(BF16)
        carried = (chosen * columns[:, slot + h:slot + h + 1]).astype(BF16)
        x_head = x_ref[now, here]
        state = state_ref[:, here]
        out = dot(jnp.concatenate([weights, carried], axis=1), jnp.concatenate([x_head, state.astype(BF16)], axis=0))
        out = out + skip_ref[h] * x_head.astype(F32)
        written = dot((b_turned * fresh[h:h + 1, :]).astype(BF16), x_head)
        state_ref[:, here] = state * kept[h:h + 1, :] + written
        z = 0.5 * z_ref[now, here].astype(F32)
        gate = z + z * jnp.tanh(z)
        part_ref[now, here] = out * gate
        gate_ref[now, here] = gate.astype(BF16)


def local_scan(meta, docs, a_log, d_skip, dt_raw, b_sel, c_rows, x_in, z_gate):
    heads, tokens = dt_raw.shape
    features = x_in.shape[1]
    chunks = tokens // LANES
    held = [pltpu.with_memory_space_constraint(v, pltpu.VMEM) for v in (dt_raw, c_rows, z_gate)]
    return pl.pallas_call(
        scan_kernel,
        grid_spec=pltpu.PrefetchScalarGridSpec(
            num_scalar_prefetch=4,
            grid=(chunks,),
            in_specs=[in_vmem()] * 5,
            out_specs=[in_vmem()] * 4,
            scratch_shapes=[
                pltpu.VMEM((LANES, features), F32),
                pltpu.VMEM((heads, LANES), F32),
                pltpu.VMEM((LANES, LANES), F32),
            ],
        ),
        out_shape=[
            pltpu.VMEM((tokens, features), F32),
            pltpu.VMEM((tokens, features), BF16),
            pltpu.VMEM((tokens, LANES), BF16),
            pltpu.VMEM((tokens, LANES), F32),
        ],
        compiler_params=params(),
        cost_estimate=pl.CostEstimate(flops=16 * LANES * tokens * features, bytes_accessed=8 * tokens * features, transcendentals=0),
        name="local_scan",
    )(meta, docs, a_log, d_skip, held[0], b_sel, held[1], x_in, held[2])


def tile_of(step, half, odd):
    return (step + (1 - odd) * half) % (2 * half)


def one_language(first, size, starts, lang_ref):
    lang = lang_at(first, starts, lang_ref)
    same = jnp.bool_(True)
    for d, s in enumerate(starts):
        inside = (s > first) & (s < first + size)
        same = same & jnp.logical_not(inside & (lang_ref[d] != lang))
    return lang, same


def has_language(which, first, size, starts, lang_ref):
    found = lang_at(first, starts, lang_ref) == which
    for d, s in enumerate(starts):
        found = found | ((s > first) & (s < first + size) & (lang_ref[d] == which))
    return found


def combine_kernel(n_states, slot, half, offset, meta, docs, c_ref, reach_ref, part_ref, gate_ref, gain_ref, down_ref, *rest):
    states, (all_gated_ref, other_ref, mine_ref, enter_ref, low_ref) = rest[:n_states], rest[n_states:]
    step = pl.program_id(0)
    tokens, features = TILE, part_ref.shape[1]
    heads = features // LANES
    tile = tile_of(step, half, meta[2])
    now = pl.ds(pl.multiple_of((offset + tile) * tokens, tokens), tokens)
    gated_ref = all_gated_ref.at[pl.ds(pl.multiple_of(tile * tokens, tokens), tokens)]
    first = meta[0] + (offset + tile) * tokens
    starts = starts_of(docs)
    lang_ref = langs_of(docs)

    if n_states > 1:
        @pl.when(step == 0)
        def _():
            total = states[0][...].astype(F32)
            for more in states[1:]:
                total = total + more[...].astype(F32)
            enter_ref[...] = total.astype(BF16)
        entering = enter_ref
    else:
        entering = states[0]

    squares = jnp.zeros((tokens, LANES), F32)
    c_low = c_ref[now, :]
    reach = reach_ref[now, :]
    pair = min(2, heads)
    for p in range(heads // pair):
        both = dot(c_low, entering[:, p * pair * LANES:(p + 1) * pair * LANES])
        for i in range(pair):
            h = p * pair + i
            here = slice(h * LANES, (h + 1) * LANES)
            entered = both[:, i * LANES:(i + 1) * LANES] * reach[:, 2 * slot + h:2 * slot + h + 1]
            gated = part_ref[now, here] + entered * gate_ref[now, here].astype(F32)
            squares = squares + gated * gated
            gated_ref[:, here] = (gated * gain_ref[:, here]).astype(BF16)

    lang, same = one_language(first, tokens, starts, lang_ref)

    @pl.when(same)
    def _():
        low_ref[...] = dot(gated_ref[...], down_ref[lang])

    @pl.when(jnp.logical_not(same))
    def _():
        low_ref[...] = jnp.zeros_like(low_ref)
        token_lang = lang_at(first + lax.broadcasted_iota(I32, (tokens, LANES), 0), starts, lang_ref)
        for k in range(down_ref.shape[0]):
            @pl.when(has_language(k, first, tokens, starts, lang_ref))
            def _():
                low_ref[...] += jnp.where(token_lang == k, dot(gated_ref[...], down_ref[k]), 0.0)

    ones = jnp.ones((8, LANES), F32)
    sums = lax.dot_general(ones, squares, (((1,), (1,)), ((), ())), precision=lax.Precision.HIGHEST, preferred_element_type=F32)
    rows = jnp.concatenate([sums[:, :LANES], sums[:, LANES:]], axis=0)

    def message(ref, at):
        ref[at, 0:tokens, :] = low_ref[...].astype(BF16)
        ref[at, tokens:tokens + SUM_ROWS, :] = rows.astype(BF16)

    @pl.when(step < half)
    def _():
        message(other_ref, step)

    @pl.when(step >= half)
    def _():
        message(mine_ref, step - half)


TILE = 2 * LANES


def combine(meta, docs, c_sel, reach, part, gate, gain, down, states, offset, tiles, slot):
    features = part.shape[1]
    half = tiles // 2
    held = [pltpu.with_memory_space_constraint(v, pltpu.VMEM) for v in [gain, down] + states]
    return pl.pallas_call(
        functools.partial(combine_kernel, len(states), slot, half, offset),
        grid_spec=pltpu.PrefetchScalarGridSpec(
            num_scalar_prefetch=2,
            grid=(tiles,),
            in_specs=[in_vmem()] * (6 + len(states)),
            out_specs=[in_vmem()] * 3,
            scratch_shapes=[
                pltpu.VMEM(states[0].shape, BF16),
                pltpu.VMEM((TILE, LANES), F32),
            ],
        ),
        out_shape=[
            pltpu.VMEM((tiles * TILE, features), BF16),
            pltpu.VMEM((half, TILE + SUM_ROWS, LANES), BF16),
            pltpu.VMEM((half, TILE + SUM_ROWS, LANES), BF16),
        ],
        compiler_params=params(),
        cost_estimate=pl.CostEstimate(flops=16 * LANES * tiles * TILE * features, bytes_accessed=8 * tiles * TILE * features, transcendentals=0),
        name="combine",
    )(meta, docs, c_sel, reach, part, gate, *held)


def finish_kernel(half, offset, all_features, meta, docs, mine_ref, other_ref, all_gated_ref, up_ref, *rest):
    out_ref = rest[-1]
    step = pl.program_id(0)
    tokens, features = TILE, all_gated_ref.shape[1]
    gated_ref = all_gated_ref.at[pl.ds(pl.multiple_of(step * tokens, tokens), tokens)]
    ranks = up_ref.shape[1]
    first = meta[0] + (offset + step) * tokens
    starts = starts_of(docs)
    lang_ref = langs_of(docs)
    is_mine = (step // half) == meta[2]
    part = step % half
    message = jnp.where(is_mine, mine_ref[part].astype(F32), other_ref[part].astype(F32))
    scale = lax.rsqrt(message[tokens:tokens + SUM_ROWS, :] / all_features + EPS)
    turned = jnp.concatenate([scale] * (LANES // SUM_ROWS), axis=0).T
    scale = jnp.concatenate([turned[:, 0:1], turned[:, 8:9]], axis=0)
    low = (message[0:tokens, :] * scale).astype(BF16)
    lang, same = one_language(first, tokens, starts, lang_ref)
    piece = min(4 * LANES, features)

    @pl.when(same)
    def _():
        for at in range(0, features, piece):
            here = slice(at, at + piece)
            lifted = dot(low, up_ref[lang, :, here])
            out_ref[:, here] = (gated_ref[:, here].astype(F32) * scale + lifted).astype(BF16)

    @pl.when(jnp.logical_not(same))
    def _():
        token_lang = lang_at(first + lax.broadcasted_iota(I32, (tokens, LANES), 0), starts, lang_ref)
        zero = jnp.zeros((), BF16)
        spread = jnp.concatenate([jnp.where(token_lang == k, low, zero) for k in range(up_ref.shape[0])], axis=1)
        for at in range(0, features, piece):
            here = slice(at, at + piece)
            lifted = dot(spread, up_ref[:, :, here].reshape(up_ref.shape[0] * ranks, piece))
            out_ref[:, here] = (gated_ref[:, here].astype(F32) * scale + lifted).astype(BF16)


def finish(meta, docs, mine, other, gated, up, offset, all_tiles, all_features, into=None):
    features = gated.shape[1]
    tiles = gated.shape[0] // TILE
    half = tiles // 2
    held = [pltpu.with_memory_space_constraint(v, pltpu.VMEM) for v in (mine, other, gated, up)]
    more = [] if into is None else [into]
    return pl.pallas_call(
        functools.partial(finish_kernel, half, offset, all_features),
        grid_spec=pltpu.PrefetchScalarGridSpec(
            num_scalar_prefetch=2,
            grid=(tiles,),
            in_specs=[in_vmem()] * 4 + [pl.BlockSpec(memory_space=pl.ANY) for _ in more],
            out_specs=pl.BlockSpec((TILE, features), lambda s, *_: (offset + s, 0)),
        ),
        out_shape=jax.ShapeDtypeStruct((all_tiles * TILE, features), BF16),
        input_output_aliases={6: 0} if more else {},
        compiler_params=params(),
        cost_estimate=pl.CostEstimate(flops=2 * LANES * tiles * TILE * features, bytes_accessed=8 * tiles * TILE * features, transcendentals=0),
        name="finish",
    )(meta, docs, *held, *more)


def sum_over_head(other, mine, devices):
    def across(v, mask):
        return lax.ppermute(v, "head", [(i, i ^ mask) for i in range(devices)])

    if devices == 1:
        return mine, other
    total = (mine.astype(F32) + across(other, 1).astype(F32)).astype(BF16)
    bit = 2
    while bit < devices:
        masks = [bit] if 2 * bit >= devices else [bit, 2 * bit, 3 * bit]
        arrived = [across(total, m) for m in masks]
        added = total.astype(F32)
        for a in arrived:
            added = added + a.astype(F32)
        total = added.astype(BF16)
        bit *= 2 ** (1 if len(masks) == 1 else 2)
    return total, across(total, 1)


def per_device(seq_size, head_size, x_in, z_gate, b_input, c_input, dt_raw, a_log, d_skip, norm_gain,
               doc_lengths, doc_lang, adapt_down, adapt_up):
    tokens, features = x_in.shape
    heads = dt_raw.shape[0]
    groups = b_input.shape[1]
    head_rank = lax.axis_index("head")
    group = head_rank * heads // (heads * head_size // groups)
    meta = jnp.stack([lax.axis_index("seq") * tokens, group, head_rank % 2]).astype(I32)
    b_rows = b_input.reshape(tokens * groups, b_input.shape[2])
    c_rows = c_input.reshape(tokens * groups, c_input.shape[2])
    longest = tokens * seq_size // LONGEST_SHARE
    hops = min(-(-(longest - 1) // tokens), seq_size - 1)

    docs = jnp.concatenate([doc_lengths, doc_lang])
    gain = norm_gain.reshape(1, features)
    all_features = features * head_size
    slot = max(8, heads)
    all_tiles = tokens // TILE
    reached = longest - 1 - (hops - 1) * tokens
    head_tiles = -(-reached // (2 * TILE)) * 2

    state, through, b_sel, x_held = block_states(meta, docs, a_log, dt_raw, b_rows, x_in)
    onward = [(i, i + 1) for i in range(seq_size - 1)]

    arrived = lax.ppermute(state, "seq", onward)
    part, gate, c_sel, reach = local_scan(meta, docs, a_log, d_skip, dt_raw, b_sel, c_rows, x_held, z_gate)
    arrived, part = lax.optimization_barrier((arrived, part))
    states = [arrived]
    for hop in range(1, hops):
        arrived = lax.ppermute((arrived.astype(F32) * through[0:1]).astype(BF16), "seq", onward)
        states.append(arrived)

    def joined(states, offset, tiles):
        return combine(meta, docs, c_sel, reach, part, gate, gain, adapt_down, states, offset, tiles, slot)

    if hops < 2 or head_tiles >= all_tiles:
        gated, other, mine = joined(states, 0, all_tiles)
        mine, other = sum_over_head(other, mine, head_size)
        return finish(meta, docs, mine, other, gated, adapt_up, 0, all_tiles, all_features)
    late, other, mine = joined(states[:-1], head_tiles, all_tiles - head_tiles)
    late_sums = sum_over_head(other, mine, head_size)
    early, other, mine = joined(states, 0, head_tiles)
    early_sums = sum_over_head(other, mine, head_size)
    out = finish(meta, docs, *late_sums, late, adapt_up, head_tiles, all_tiles, all_features)
    return finish(meta, docs, *early_sums, early, adapt_up, 0, all_tiles, all_features, out)


def solution(mesh):
    placed = (
        P("seq", "head"),
        P("seq", "head"),
        P("seq", None, None),
        P("seq", None, None),
        P("head", "seq"),
        P("head"),
        P("head"),
        P("head"),
        P(),
        P(),
        P(None, "head", None),
        P(None, None, "head"),
    )
    return jax.shard_map(
        functools.partial(per_device, mesh.shape["seq"], mesh.shape["head"]),
        mesh=mesh, in_specs=placed, out_specs=P("seq", "head"), check_vma=False,
    )
```

time: 78.9 us -> 63.7 us (0.81); the launches traced: 77.4 us -> 63.4 us
  waiting for transfers between devices: 20 us -> 10.6 us
  Pallas kernels: 40.1 us -> 34.7 us
  local copies, waits for them, and re-layouts: 3.78 us -> 0.7 us
  starting transfers between devices: 13 us -> 16 us
    ppermute x5 -> x10, waiting for transfers between devices: 8.92 us -> 3.67 us  [across(): return lax.ppermute(v, 'head', [(i, i ^ mask) for i in range(devices)])]
    ppermute x2, waiting for transfers between devices: 11.1 us -> 6.98 us  [the longest x1 6.98 us: per_device(): lax.ppermute((arrived.astype(F32) * through[0:1]).astype(BF16), 'seq', on...]
    ppermute x5 -> x10, starting transfers between devices: 3.63 us -> 7.39 us  [across(): return lax.ppermute(v, 'head', [(i, i ^ mask) for i in range(devices)])]
    pallas_call x1, Pallas kernels: 18.4 us -> 14.8 us  [local_scan(): pl.pallas_call(scan_kernel, grid_spec=pltpu.PrefetchScalarGridSpec(num_sc...]
    unnamed x20 -> x16, local copies, waits for them, and re-layouts: 3.77 us -> 0.69 us
    pallas_call x1 -> x2, Pallas kernels: 9.89 us -> 7.68 us  [combine(): pl.pallas_call(functools.partial(combine_kernel, len(states), slot, half,...]
    pallas_call x1 -> x2, Pallas kernels: 6.52 us -> 6.15 us  [finish(): pl.pallas_call(functools.partial(finish_kernel, half, offset, all_feature...]
  transfers between devices with their start and end apart: 7 -> 12, of which waited for: 6 -> 5; matrix products, arithmetic and copies ran while one was open for 0% -> 0% of each run, Pallas kernels for 24% -> 40%
where the time goes in v2:
time: 63.7 us; the launch traced here: 63.4 us
  Pallas kernels  34.7 us (54%)
  starting transfers between devices  16 us (25%)
  waiting for transfers between devices  10.6 us (17%)
  other arithmetic  1.08 us (2%)
  local copies, waits for them, and re-layouts  0.7 us (1%)
    pallas_call x1, Pallas kernels, local_scan(): pl.pallas_call(scan_kernel, grid_spec=pltpu.PrefetchScalarGridSpec(num_sc...  14.8 us
    pallas_call x2, Pallas kernels, combine(): pl.pallas_call(functools.partial(combine_kernel, len(states), slot, half,...  7.68 us
    ppermute x10, starting transfers between devices, across(): return lax.ppermute(v, 'head', [(i, i ^ mask) for i in range(devices)])  7.39 us
    ppermute x1, waiting for transfers between devices, per_device(): lax.ppermute((arrived.astype(F32) * through[0:1]).astype(BF16), 'seq', on...  6.98 us
    pallas_call x2, Pallas kernels, finish(): pl.pallas_call(functools.partial(finish_kernel, half, offset, all_feature...  6.15 us
    pallas_call x1, Pallas kernels, block_states(): pl.pallas_call(functools.partial(state_kernel, x_parts, b_parts), grid_sp...  6.05 us
    ppermute x1, starting transfers between devices, per_device(): arrived = lax.ppermute(state, 'seq', onward)  4.96 us
    ppermute x1, starting transfers between devices, per_device(): lax.ppermute((arrived.astype(F32) * through[0:1]).astype(BF16), 'seq', on...  3.67 us
  transfers between devices with their start and end apart: 12, of which 5 were waited for; matrix products, arithmetic and copies ran while one was open for 0% of the time, Pallas kernels for 40%

profile of v2, /device:TPU:0, one launch (start us, length us, event | category | flops | bytes accessed | tf_op | source)
XLA Modules:
  0.0 63.4 jit_solution(13918335935201413355)
XLA Ops:
  0.0 0.8 %pad_add_fusion.1.docs = s32[12]{0:T(128)S(1)} fusion(s32[6]{0:T(128)} %param.21, s32[6]{0:T(128)} %param.20), kind=kLoop, calls=%fused_computation.6 | loop fusion | flops 12 | bytes 96 | tf_op jit(solution)/shard_map/concatenate | solution.py:495
  0.8 0.1 pad_add_fusion.meta
  0.9 0.7 %copy-done.4 = f32[16]{0:T(128)S(1)} copy-done((f32[16]{0:T(128)S(1)}, f32[16]{0:T(128)}, u32[]{:S(2)}) %copy-start.4) | copy-done | bytes 88
  1.5 6.0 %block_states.1 = (bf16[128,2048]{1,0:T(8,128)(2,1)S(1)}, f32[8,2048]{1,0:T(8,128)S(1)}, bf16[1024,128]{1,0:T(8,128)(2,1)S(1)}, bf16[1024,2048]{1,0:T(8,128)(2,1)S(1)}) custom-call(s32[3]{0:T(128)S(1)} %pad_add_fusion.meta, s32[12]{0:T(128)S(1)} %pad_add_fusion.1.docs, f32[16]{0:T(128)S(1)} %copy-done.4, f32[16,1024]{1,0:T(8,128)} %dt_ref.1, ...), custom_call_target="tpu_custom_call" | custom-call | flops 536870912 | bytes 16777216 | tf_op jit(solution)/shard_map/block_states/pallas_call | solution.py:158
  7.6 5.0 %collective-permute-start = (bf16[128,2048]{1,0:T(8,128)(2,1)S(1)}, bf16[128,2048]{1,0:T(8,128)(2,1)S(1)}, u32[]{:S(2)}, u32[]{:S(2)}) collective-permute-start(bf16[128,2048]{1,0:T(8,128)(2,1)S(1)} %get-tuple-element.25), channel_id=1, source_target_pairs={{0,8},{8,16},{16,24},{1,9},{9,17},{17,25},{2,10},{10,18},{18,26},{... | collective-permute-start | bytes 1572872 | tf_op jit(solution)/shard_map/ppermute | solution.py:506
  12.6 0.0 copy-start
  12.6 0.0 copy-start.3
  12.6 14.8 %local_scan.1 = (f32[1024,2048]{1,0:T(8,128)S(1)}, bf16[1024,2048]{1,0:T(8,128)(2,1)S(1)}, bf16[1024,128]{1,0:T(8,128)(2,1)S(1)}, f32[1024,128]{1,0:T(8,128)S(1)}) custom-call(s32[3]{0:T(128)S(1)} %pad_add_fusion.meta, s32[12]{0:T(128)S(1)} %pad_add_fusion.1.docs, f32[16]{0:T(128)S(1)} %copy-done.4, f32[16]{0:T(128)S(1)} %copy-done.7, ...), custom_call_target="tpu_custom_call" | custom-call | flops 4294967296 | bytes 16777216 | tf_op jit(solution)/shard_map/local_scan/pallas_call | solution.py:260
  27.4 0.0 collective-permute-done.rest_0_
  27.4 0.1 multiply_convert_fusion
  27.5 3.7 %collective-permute-start.1 = (bf16[128,2048]{1,0:T(8,128)(2,1)S(1)}, bf16[128,2048]{1,0:T(8,128)(2,1)S(1)}, u32[]{:S(2)}, u32[]{:S(2)}) collective-permute-start(bf16[128,2048]{1,0:T(8,128)(2,1)S(1)} %multiply_convert_fusion), channel_id=1, source_target_pairs={{0,8},{8,16},{16,24},{1,9},{9,17},{17,25},{2,10},{10,18},{18,26},{... | collective-permute-start | bytes 1572872 | tf_op jit(solution)/shard_map/ppermute | solution.py:511
  31.2 3.6 %combine.3 = (bf16[512,2048]{1,0:T(8,128)(2,1)S(1)}, bf16[1,272,128]{2,1,0:T(8,128)(2,1)S(1)}, bf16[1,272,128]{2,1,0:T(8,128)(2,1)S(1)}) custom-call(s32[3]{0:T(128)S(1)} %pad_add_fusion.meta, s32[12]{0:T(128)S(1)} %pad_add_fusion.1.docs, bf16[1024,128]{1,0:T(8,128)(2,1)S(1)} %get-tuple-element.23.c_ref, f32[1024,128]{1,0:T(8,128)S(1)} %get-tuple-element.24.reach_ref, ...), custom_call_target="tpu_custom_call" | custom-call | flops 2147483648 | bytes 8388608 | tf_op jit(solution)/shard_map/combine/pallas_call | solution.py:381
  34.8 0.0 copy-start.1
  34.8 0.1 collective-permute-start.7
  34.9 7.0 %collective-permute-done.1.rest_1_ = bf16[128,2048]{1,0:T(8,128)(2,1)S(1)} collective-permute-done((bf16[128,2048]{1,0:T(8,128)(2,1)S(1)}, bf16[128,2048]{1,0:T(8,128)(2,1)S(1)}, u32[]{:S(2)}, u32[]{:S(2)}) %collective-permute-start.1) | collective-permute-done | bytes 524320 | tf_op jit(solution)/shard_map/ppermute | solution.py:511
  41.9 4.1 %combine.2 = (bf16[512,2048]{1,0:T(8,128)(2,1)S(1)}, bf16[1,272,128]{2,1,0:T(8,128)(2,1)S(1)}, bf16[1,272,128]{2,1,0:T(8,128)(2,1)S(1)}) custom-call(s32[3]{0:T(128)S(1)} %pad_add_fusion.meta, s32[12]{0:T(128)S(1)} %pad_add_fusion.1.docs, bf16[1024,128]{1,0:T(8,128)(2,1)S(1)} %get-tuple-element.23.c_ref, f32[1024,128]{1,0:T(8,128)S(1)} %get-tuple-element.24.reach_ref, ...), custom_call_target="tpu_custom_call" | custom-call | flops 2147483648 | bytes 8388608 | tf_op jit(solution)/shard_map/combine/pallas_call | solution.py:381
  46.0 0.1 collective-permute-start.2
  46.1 0.0 collective-permute-done.7
  46.1 2.5 %collective-permute-start.10 = (bf16[1,272,128]{2,1,0:T(8,128)(2,1)S(1)}, bf16[1,272,128]{2,1,0:T(8,128)(2,1)S(1)}, u32[]{:S(2)}, u32[]{:S(2)}) collective-permute-start(bf16[1,272,128]{2,1,0:T(8,128)(2,1)S(1)} %add_convert_fusion.1), channel_id=1, source_target_pairs={{0,6},{1,7},{2,4},{3,5},{4,2},{5,3},{6,0},{7,1},{8,14},{9,15},{10,... | collective-permute-start | bytes 208904 | tf_op jit(solution)/shard_map/ppermute | solution.py:465
  48.6 0.5 collective-permute-start.9
  49.2 0.5 collective-permute-start.8
  49.7 2.5 %collective-permute-start.5 = (bf16[1,272,128]{2,1,0:T(8,128)(2,1)S(1)}, bf16[1,272,128]{2,1,0:T(8,128)(2,1)S(1)}, u32[]{:S(2)}, u32[]{:S(2)}) collective-permute-start(bf16[1,272,128]{2,1,0:T(8,128)(2,1)S(1)} %add_convert_fusion.3), channel_id=1, source_target_pairs={{0,6},{1,7},{2,4},{3,5},{4,2},{5,3},{6,0},{7,1},{8,14},{9,15},{10,... | collective-permute-start | bytes 208904 | tf_op jit(solution)/shard_map/ppermute | solution.py:465
  52.2 0.5 collective-permute-start.4
  52.7 0.5 collective-permute-start.3
  53.3 0.7 %collective-permute-done.8 = bf16[1,272,128]{2,1,0:T(8,128)(2,1)S(1)} collective-permute-done((bf16[1,272,128]{2,1,0:T(8,128)(2,1)S(1)}, bf16[1,272,128]{2,1,0:T(8,128)(2,1)S(1)}, u32[]{:S(2)}, u32[]{:S(2)}) %collective-permute-start.8) | collective-permute-done | bytes 69664 | tf_op jit(solution)/shard_map/ppermute | solution.py:465
  54.0 0.1 collective-permute-start.11
  54.1 1.7 %collective-permute-done.5 = bf16[1,272,128]{2,1,0:T(8,128)(2,1)S(1)} collective-permute-done((bf16[1,272,128]{2,1,0:T(8,128)(2,1)S(1)}, bf16[1,272,128]{2,1,0:T(8,128)(2,1)S(1)}, u32[]{:S(2)}, u32[]{:S(2)}) %collective-permute-start.5) | collective-permute-done | bytes 69664 | tf_op jit(solution)/shard_map/ppermute | solution.py:465
  55.8 0.8 %collective-permute-done.4 = bf16[1,272,128]{2,1,0:T(8,128)(2,1)S(1)} collective-permute-done((bf16[1,272,128]{2,1,0:T(8,128)(2,1)S(1)}, bf16[1,272,128]{2,1,0:T(8,128)(2,1)S(1)}, u32[]{:S(2)}, u32[]{:S(2)}) %collective-permute-start.4) | collective-permute-done | bytes 69664 | tf_op jit(solution)/shard_map/ppermute | solution.py:465
  56.6 0.4 collective-permute-done.3
  57.1 0.1 collective-permute-start.6
  57.2 2.9 %finish.2.rest_0_ = bf16[1024,2048]{1,0:T(8,128)(2,1)} custom-call(s32[3]{0:T(128)S(1)} %pad_add_fusion.meta, s32[12]{0:T(128)S(1)} %pad_add_fusion.1.docs, bf16[1,272,128]{2,1,0:T(8,128)(2,1)S(1)} %add_convert_fusion.mine_ref, bf16[1,272,128]{2,1,0:T(8,128)(2,1)S(1)} %collective-permute-done.11.other_ref, ...), custom_call_target="tpu_custom_call" | custom-call | flops 268435456 | bytes 8388608 | tf_op jit(solution)/shard_map/finish/pallas_call | solution.py:447
  60.1 3.2 %finish.3 = bf16[1024,2048]{1,0:T(8,128)(2,1)} custom-call(s32[3]{0:T(128)S(1)} %pad_add_fusion.meta, s32[12]{0:T(128)S(1)} %pad_add_fusion.1.docs, bf16[1,272,128]{2,1,0:T(8,128)(2,1)S(1)} %add_convert_fusion.2.mine_ref, bf16[1,272,128]{2,1,0:T(8,128)(2,1)S(1)} %collective-permute-done.6.other_ref, ...), custom_call_target="tpu_custom_call", output_to_operand_aliasing={{}: (6, {})} | custom-call | flops 268435456 | bytes 8388608 | tf_op jit(solution)/shard_map/finish/pallas_call | solution.py:447
  (22 shorter events, 0.2 us)
Async XLA Ops:
  0.0 12.6 %copy-start.2 = (f32[16,1024]{1,0:T(8,128)S(1)}, f32[16,1024]{1,0:T(8,128)}, u32[]{:S(2)}) copy-start(f32[16,1024]{1,0:T(8,128)} %dt_ref.1) | copy-start | bytes 196612
  0.0 12.6 %copy-start.7 = (f32[16]{0:T(128)S(1)}, f32[16]{0:T(128)}, u32[]{:S(2)}) copy-start(f32[16]{0:T(128)} %skip_ref.1) | copy-start | bytes 196
  0.9 0.7 %copy-start.4 = (f32[16]{0:T(128)S(1)}, f32[16]{0:T(128)}, u32[]{:S(2)}) copy-start(f32[16]{0:T(128)} %alog_ref.3) | copy-start | bytes 196
  1.5 11.1 %copy-start.5 = (bf16[1024,2048]{1,0:T(8,128)(2,1)S(1)}, bf16[1024,2048]{1,0:T(8,128)(2,1)}, u32[]{:S(2)}) copy-start(bf16[1024,2048]{1,0:T(8,128)(2,1)} %z_ref.1) | copy-start | bytes 12582916
  1.5 11.1 %copy-start.6 = (bf16[1024,8,128]{2,1,0:T(8,128)(2,1)S(1)}, bf16[1024,8,128]{2,1,0:T(8,128)(2,1)}, u32[]{:S(2)}) copy-start(bf16[1024,8,128]{2,1,0:T(8,128)(2,1)} %param.15) | copy-start | bytes 6291460
  7.6 19.9 %collective-permute-start = (bf16[128,2048]{1,0:T(8,128)(2,1)S(1)}, bf16[128,2048]{1,0:T(8,128)(2,1)S(1)}, u32[]{:S(2)}, u32[]{:S(2)}) collective-permute-start(bf16[128,2048]{1,0:T(8,128)(2,1)S(1)} %get-tuple-element.25), channel_id=1, source_target_pairs={{0,8},{8,16},{16,24},{1,9},{9,17},{17,25},{2,10},{10,18},{18,26},{... | collective-permute-start | bytes 1572872 | tf_op jit(solution)/shard_map/ppermute | solution.py:506
  12.6 18.6 %copy-start = (bf16[4,2048,128]{2,1,0:T(8,128)(2,1)S(1)}, bf16[4,2048,128]{2,1,0:T(8,128)(2,1)}, u32[]{:S(2)}) copy-start(bf16[4,2048,128]{2,1,0:T(8,128)(2,1)} %down_ref.3) | copy-start | bytes 6291460
  12.6 18.6 %copy-start.3 = (f32[2048]{0:T(1024)S(1)}, f32[2048]{0:T(1024)}, u32[]{:S(2)}) copy-start(f32[2048]{0:T(1024)} %param.19) | copy-start | bytes 24580
  27.5 14.3 %collective-permute-start.1 = (bf16[128,2048]{1,0:T(8,128)(2,1)S(1)}, bf16[128,2048]{1,0:T(8,128)(2,1)S(1)}, u32[]{:S(2)}, u32[]{:S(2)}) collective-permute-start(bf16[128,2048]{1,0:T(8,128)(2,1)S(1)} %multiply_convert_fusion), channel_id=1, source_target_pairs={{0,8},{8,16},{16,24},{1,9},{9,17},{17,25},{2,10},{10,18},{18,26},{... | collective-permute-start | bytes 1572872 | tf_op jit(solution)/shard_map/ppermute | solution.py:511
  34.8 22.4 %copy-start.1 = (bf16[4,128,2048]{2,1,0:T(8,128)(2,1)S(1)}, bf16[4,128,2048]{2,1,0:T(8,128)(2,1)}, u32[]{:S(2)}) copy-start(bf16[4,128,2048]{2,1,0:T(8,128)(2,1)} %up_ref.3) | copy-start | bytes 6291460
  34.8 11.3 %collective-permute-start.7 = (bf16[1,272,128]{2,1,0:T(8,128)(2,1)S(1)}, bf16[1,272,128]{2,1,0:T(8,128)(2,1)S(1)}, u32[]{:S(2)}, u32[]{:S(2)}) collective-permute-start(bf16[1,272,128]{2,1,0:T(8,128)(2,1)S(1)} %get-tuple-element.35), channel_id=1, source_target_pairs={{0,1},{1,0},{2,3},{3,2},{4,5},{5,4},{6,7},{7,6},{8,9},{9,8},{10,11... | collective-permute-start | bytes 208904 | tf_op jit(solution)/shard_map/ppermute | solution.py:465
  46.0 3.7 %collective-permute-start.2 = (bf16[1,272,128]{2,1,0:T(8,128)(2,1)S(1)}, bf16[1,272,128]{2,1,0:T(8,128)(2,1)S(1)}, u32[]{:S(2)}, u32[]{:S(2)}) collective-permute-start(bf16[1,272,128]{2,1,0:T(8,128)(2,1)S(1)} %get-tuple-element.32), channel_id=1, source_target_pairs={{0,1},{1,0},{2,3},{3,2},{4,5},{5,4},{6,7},{7,6},{8,9},{9,8},{10,11... | collective-permute-start | bytes 208904 | tf_op jit(solution)/shard_map/ppermute | solution.py:465
  46.1 6.6 %collective-permute-start.10 = (bf16[1,272,128]{2,1,0:T(8,128)(2,1)S(1)}, bf16[1,272,128]{2,1,0:T(8,128)(2,1)S(1)}, u32[]{:S(2)}, u32[]{:S(2)}) collective-permute-start(bf16[1,272,128]{2,1,0:T(8,128)(2,1)S(1)} %add_convert_fusion.1), channel_id=1, source_target_pairs={{0,6},{1,7},{2,4},{3,5},{4,2},{5,3},{6,0},{7,1},{8,14},{9,15},{10,... | collective-permute-start | bytes 208904 | tf_op jit(solution)/shard_map/ppermute | solution.py:465
  48.6 4.6 %collective-permute-start.9 = (bf16[1,272,128]{2,1,0:T(8,128)(2,1)S(1)}, bf16[1,272,128]{2,1,0:T(8,128)(2,1)S(1)}, u32[]{:S(2)}, u32[]{:S(2)}) collective-permute-start(bf16[1,272,128]{2,1,0:T(8,128)(2,1)S(1)} %add_convert_fusion.1), channel_id=1, source_target_pairs={{0,4},{1,5},{2,6},{3,7},{4,0},{5,1},{6,2},{7,3},{8,12},{9,13},{10,... | collective-permute-start | bytes 208904 | tf_op jit(solution)/shard_map/ppermute | solution.py:465
  49.2 4.8 %collective-permute-start.8 = (bf16[1,272,128]{2,1,0:T(8,128)(2,1)S(1)}, bf16[1,272,128]{2,1,0:T(8,128)(2,1)S(1)}, u32[]{:S(2)}, u32[]{:S(2)}) collective-permute-start(bf16[1,272,128]{2,1,0:T(8,128)(2,1)S(1)} %add_convert_fusion.1), channel_id=1, source_target_pairs={{0,2},{1,3},{2,0},{3,1},{4,6},{5,7},{6,4},{7,5},{8,10},{9,11},{10,... | collective-permute-start | bytes 208904 | tf_op jit(solution)/shard_map/ppermute | solution.py:465
  49.7 6.1 %collective-permute-start.5 = (bf16[1,272,128]{2,1,0:T(8,128)(2,1)S(1)}, bf16[1,272,128]{2,1,0:T(8,128)(2,1)S(1)}, u32[]{:S(2)}, u32[]{:S(2)}) collective-permute-start(bf16[1,272,128]{2,1,0:T(8,128)(2,1)S(1)} %add_convert_fusion.3), channel_id=1, source_target_pairs={{0,6},{1,7},{2,4},{3,5},{4,2},{5,3},{6,0},{7,1},{8,14},{9,15},{10,... | collective-permute-start | bytes 208904 | tf_op jit(solution)/shard_map/ppermute | solution.py:465
  52.2 4.4 %collective-permute-start.4 = (bf16[1,272,128]{2,1,0:T(8,128)(2,1)S(1)}, bf16[1,272,128]{2,1,0:T(8,128)(2,1)S(1)}, u32[]{:S(2)}, u32[]{:S(2)}) collective-permute-start(bf16[1,272,128]{2,1,0:T(8,128)(2,1)S(1)} %add_convert_fusion.3), channel_id=1, source_target_pairs={{0,4},{1,5},{2,6},{3,7},{4,0},{5,1},{6,2},{7,3},{8,12},{9,13},{10,... | collective-permute-start | bytes 208904 | tf_op jit(solution)/shard_map/ppermute | solution.py:465
  52.7 4.3 %collective-permute-start.3 = (bf16[1,272,128]{2,1,0:T(8,128)(2,1)S(1)}, bf16[1,272,128]{2,1,0:T(8,128)(2,1)S(1)}, u32[]{:S(2)}, u32[]{:S(2)}) collective-permute-start(bf16[1,272,128]{2,1,0:T(8,128)(2,1)S(1)} %add_convert_fusion.3), channel_id=1, source_target_pairs={{0,2},{1,3},{2,0},{3,1},{4,6},{5,7},{6,4},{7,5},{8,10},{9,11},{10,... | collective-permute-start | bytes 208904 | tf_op jit(solution)/shard_map/ppermute | solution.py:465
  54.0 3.2 %collective-permute-start.11 = (bf16[1,272,128]{2,1,0:T(8,128)(2,1)S(1)}, bf16[1,272,128]{2,1,0:T(8,128)(2,1)S(1)}, u32[]{:S(2)}, u32[]{:S(2)}) collective-permute-start(bf16[1,272,128]{2,1,0:T(8,128)(2,1)S(1)} %add_convert_fusion.mine_ref), channel_id=1, source_target_pairs={{0,1},{1,0},{2,3},{3,2},{4,5},{5,4},{6,7},{7,6},{8,9},{9,8},{10,11... | collective-permute-start | bytes 208904 | tf_op jit(solution)/shard_map/ppermute | solution.py:465
  57.1 3.0 %collective-permute-start.6 = (bf16[1,272,128]{2,1,0:T(8,128)(2,1)S(1)}, bf16[1,272,128]{2,1,0:T(8,128)(2,1)S(1)}, u32[]{:S(2)}, u32[]{:S(2)}) collective-permute-start(bf16[1,272,128]{2,1,0:T(8,128)(2,1)S(1)} %add_convert_fusion.2.mine_ref), channel_id=1, source_target_pairs={{0,1},{1,0},{2,3},{3,2},{4,5},{5,4},{6,7},{7,6},{8,9},{9,8},{10,11... | collective-permute-start | bytes 208904 | tf_op jit(solution)/shard_map/ppermute | solution.py:465

commit v3 on v2

v3 whole, which is shorter than its diff:
```python
import functools

import jax
import jax.numpy as jnp
from jax import lax
from jax.experimental import pallas as pl
from jax.experimental.pallas import tpu as pltpu
from jax.sharding import PartitionSpec as P

F32 = jnp.float32
BF16 = jnp.bfloat16
I32 = jnp.int32
LOG2E = 1.4426950408889634
EPS = 1e-05
LANES = 128
LONGEST_SHARE = 3
VMEM_LIMIT = 16 * 1024 * 1024


def params():
    return pltpu.CompilerParams(vmem_limit_bytes=VMEM_LIMIT)


def starts_of(len_ref):
    starts, at = [], jnp.int32(0)
    for d in range(len_ref.shape[0]):
        starts.append(at)
        at = at + len_ref[d]
    return starts


def doc_at(pos, starts):
    found = jnp.where(pos >= starts[0], 0, -1)
    for s in starts[1:]:
        found = found + jnp.where(pos >= s, 1, 0)
    return found


def lang_at(pos, starts, lang_ref):
    found = jnp.where(pos >= 0, lang_ref[0], 0)
    for d in range(1, len(starts)):
        found = jnp.where(pos >= starts[d], lang_ref[d], found)
    return found


def rates(alog_ref, rows):
    which = lax.broadcasted_iota(I32, (rows, LANES), 0)
    column = jnp.zeros((rows, LANES), F32)
    for h in range(rows):
        column = jnp.where(which == h, alog_ref[h], column)
    return -LOG2E * jnp.exp(column)


def softplus(v):
    return jnp.maximum(v, 0.0) + jnp.log(1.0 + jnp.exp(-jnp.abs(v)))


def running(v, back):
    width = v.shape[1]
    lane = lax.broadcasted_iota(I32, v.shape, 1)
    step = 1
    while step < width:
        if back:
            v = v + jnp.where(lane + step < width, pltpu.roll(v, width - step, 1), 0.0)
        else:
            v = v + jnp.where(lane >= step, pltpu.roll(v, step, 1), 0.0)
        step *= 2
    return v


def pick_matrix(group, groups):
    shape = (LANES, LANES * groups)
    row = lax.broadcasted_iota(I32, shape, 0)
    col = lax.broadcasted_iota(I32, shape, 1)
    return jnp.where(col == row * groups + group, 1.0, 0.0).astype(BF16)


def dot(a, b):
    return jnp.dot(a, b, preferred_element_type=F32)


def group_of(head_rank, heads, head_size, groups):
    return head_rank * heads // (heads * head_size // groups)


def state_kernel(head_size, len_hbm, alog_hbm, dt_hbm, b_hbm, x_hbm, state_ref, thr_ref, bsel_ref, bt_ref, x_ref,
                 len_ref, alog_ref, dt_ref, b_ref, w_ref, all_ref, sems):
    heads, tokens = dt_ref.shape
    groups = b_ref.shape[0] // tokens
    copies = [
        pltpu.make_async_copy(source, target, sems.at[i])
        for i, (source, target) in enumerate([
            (dt_hbm, dt_ref), (len_hbm, len_ref), (alog_hbm, alog_ref), (b_hbm, b_ref), (x_hbm, x_ref),
        ])
    ]
    for copy in copies:
        copy.start()
    for copy in copies[:3]:
        copy.wait()

    starts = starts_of(len_ref)
    base = lax.axis_index("seq") * tokens
    rate = rates(alog_ref, heads)
    parts, totals = [], []
    for c in range(tokens // LANES):
        step_dt = softplus(dt_ref[:, c * LANES:(c + 1) * LANES])
        decay = step_dt * rate
        after = running(decay, True)
        parts.append((step_dt, after - decay))
        totals.append(after[:, 0:1])
    last_doc = doc_at(base + tokens - 1, starts)
    first_doc = doc_at(base - 1, starts)
    later = jnp.zeros((heads, 1), F32)
    for c in reversed(range(tokens // LANES)):
        step_dt, inside = parts[c]
        pos = base + c * LANES + lax.broadcasted_iota(I32, (heads, LANES), 1)
        alive = doc_at(pos, starts) == last_doc
        w_ref[:, c * LANES:(c + 1) * LANES] = jnp.where(alive, jnp.exp2(inside + later) * step_dt, 0.0)
        later = later + totals[c]
    kept = jnp.where(last_doc == first_doc, 1.0, 0.0)
    all_ref[...] = jnp.broadcast_to(jnp.exp2(later) * kept, all_ref.shape)
    for h in range(heads):
        thr_ref[:, h * LANES:(h + 1) * LANES] = jnp.broadcast_to(all_ref[h:h + 1, :], (8, LANES))

    pick = pick_matrix(group_of(lax.axis_index("head"), heads, head_size, groups), groups)
    copies[3].wait()
    for c in range(tokens // LANES):
        here = slice(c * LANES, (c + 1) * LANES)
        chosen = dot(pick, b_ref[c * LANES * groups:(c + 1) * LANES * groups, :])
        bsel_ref[here, :] = chosen.astype(BF16)
        bt_ref[:, here] = chosen.T.astype(BF16)

    copies[4].wait()
    for h in range(heads):
        here = slice(h * LANES, (h + 1) * LANES)
        weighted = bt_ref[...] * w_ref[h:h + 1, :].astype(BF16)
        state_ref[:, here] = dot(weighted, x_ref[:, here]).astype(BF16)


def in_vmem():
    return pl.BlockSpec(memory_space=pltpu.VMEM)


def block_states(head_size, doc_lengths, a_log, dt_raw, b_rows, x_in):
    heads, tokens = dt_raw.shape
    features = x_in.shape[1]
    return pl.pallas_call(
        functools.partial(state_kernel, head_size),
        grid_spec=pltpu.PrefetchScalarGridSpec(
            num_scalar_prefetch=0,
            grid=(1,),
            in_specs=[pl.BlockSpec(memory_space=pl.ANY)] * 5,
            out_specs=[in_vmem()] * 5,
            scratch_shapes=[
                pltpu.SMEM(doc_lengths.shape, I32),
                pltpu.SMEM(a_log.shape, F32),
                pltpu.VMEM((heads, tokens), F32),
                pltpu.VMEM(b_rows.shape, BF16),
                pltpu.VMEM((heads, tokens), F32),
                pltpu.VMEM((heads, LANES), F32),
                pltpu.SemaphoreType.DMA((5,)),
            ],
        ),
        out_shape=[
            pltpu.VMEM((LANES, features), BF16),
            pltpu.VMEM((8, features), F32),
            pltpu.VMEM((tokens, LANES), BF16),
            pltpu.VMEM((LANES, tokens), BF16),
            pltpu.VMEM((tokens, features), BF16),
        ],
        compiler_params=params(),
        cost_estimate=pl.CostEstimate(flops=2 * LANES * tokens * features, bytes_accessed=8 * tokens * features, transcendentals=0),
        name="block_states",
    )(*[pltpu.with_memory_space_constraint(v, pltpu.HBM) for v in (doc_lengths, a_log, dt_raw, b_rows, x_in)])


def scan_kernel(head_size, len_ref, alog_ref, skip_ref, dt_ref, b_ref, bt_ref, c_ref, x_ref, z_ref,
                part_ref, gate_ref, csel_ref, reach_ref, state_ref, before_ref, fresh_ref, kept_ref, scores_ref, stack_ref):
    step = pl.program_id(0)
    heads, tokens = dt_ref.shape
    groups = c_ref.shape[0] // tokens
    slot = max(8, heads)

    @pl.when(step == 0)
    def _():
        state_ref[...] = jnp.zeros_like(state_ref)
        stack_ref[...] = jnp.zeros_like(stack_ref)
        starts = starts_of(len_ref)
        block = lax.axis_index("seq") * tokens
        rate = rates(alog_ref, heads)
        pick = pick_matrix(group_of(lax.axis_index("head"), heads, head_size, groups), groups)
        past = jnp.zeros((heads, LANES), F32)
        doc_block = doc_at(block - 1, starts)
        for c in range(tokens // LANES):
            here = slice(c * LANES, (c + 1) * LANES)
            base = block + c * LANES
            step_dt = softplus(dt_ref[:, here])
            total_to = running(step_dt * rate, False)
            chunk_total = jnp.broadcast_to(total_to[:, LANES - 1:LANES], (heads, LANES))
            before_ref[:, here] = total_to - jnp.log(step_dt) * LOG2E
            doc = doc_at(base + lax.broadcasted_iota(I32, (heads, LANES), 1), starts)
            doc_in = doc_at(base - 1, starts)
            doc_out = doc_at(base + LANES - 1, starts)
            fresh_ref[:, here] = jnp.where(doc == doc_out, jnp.exp2(chunk_total - total_to) * step_dt, 0.0)
            kept_ref[c] = jnp.exp2(chunk_total) * jnp.where(doc_in == doc_out, 1.0, 0.0)
            stack_ref[c, 0:heads, :] = total_to
            stack_ref[c, slot:slot + heads, :] = jnp.where(doc == doc_in, jnp.exp2(total_to), 0.0)
            stack_ref[c, 2 * slot:2 * slot + heads, :] = jnp.where(doc == doc_block, jnp.exp2(past + total_to), 0.0)
            past = past + chunk_total
            reach_ref[here, :] = stack_ref[c].T
            row_pos = base + lax.broadcasted_iota(I32, (LANES, LANES), 0)
            col_pos = base + lax.broadcasted_iota(I32, (LANES, LANES), 1)
            keep = (row_pos >= col_pos) & (doc_at(row_pos, starts) == doc_at(col_pos, starts))
            c_low = dot(pick, c_ref[c * LANES * groups:(c + 1) * LANES * groups, :]).astype(BF16)
            csel_ref[here, :] = c_low
            scores = lax.dot_general(c_low, b_ref[here, :], (((1,), (1,)), ((), ())), preferred_element_type=F32)
            scores_ref[c] = jnp.where(keep, scores, 0.0)

    now = pl.ds(pl.multiple_of(step * LANES, LANES), LANES)
    columns = reach_ref[now, :]
    chosen = csel_ref[now, :]
    before = before_ref[:, now]
    fresh = fresh_ref[:, now].astype(BF16)
    kept = kept_ref[step]
    scores = scores_ref[step]
    b_turned = bt_ref[:, now]

    for h in range(heads):
        here = slice(h * LANES, (h + 1) * LANES)
        gaps = jnp.minimum(columns[:, h:h + 1] - before[h:h + 1, :], 80.0)
        weights = (jnp.exp2(gaps) * scores).astype(BF16)
        carried = chosen * columns[:, slot + h:slot + h + 1].astype(BF16)
        x_head = x_ref[now, here]
        state = state_ref[:, here]
        out = dot(jnp.concatenate([weights, carried], axis=1), jnp.concatenate([x_head, state.astype(BF16)], axis=0))
        out = out + skip_ref[h] * x_head.astype(F32)
        written = dot(b_turned * fresh[h:h + 1, :], x_head)
        state_ref[:, here] = state * kept[h:h + 1, :] + written
        z = 0.5 * z_ref[now, here].astype(F32)
        gate = z + z * jnp.tanh(z)
        part_ref[now, here] = out * gate
        gate_ref[now, here] = gate.astype(BF16)


def local_scan(head_size, doc_lengths, a_log, d_skip, dt_raw, b_sel, b_turned, c_rows, x_in, z_gate):
    heads, tokens = dt_raw.shape
    features = x_in.shape[1]
    chunks = tokens // LANES
    held = [pltpu.with_memory_space_constraint(v, pltpu.VMEM) for v in (dt_raw, c_rows, z_gate)]
    return pl.pallas_call(
        functools.partial(scan_kernel, head_size),
        grid_spec=pltpu.PrefetchScalarGridSpec(
            num_scalar_prefetch=3,
            grid=(chunks,),
            in_specs=[in_vmem()] * 6,
            out_specs=[in_vmem()] * 4,
            scratch_shapes=[
                pltpu.VMEM((LANES, features), F32),
                pltpu.VMEM((heads, tokens), F32),
                pltpu.VMEM((heads, tokens), F32),
                pltpu.VMEM((chunks, heads, LANES), F32),
                pltpu.VMEM((chunks, LANES, LANES), F32),
                pltpu.VMEM((chunks, LANES, LANES), F32),
            ],
        ),
        out_shape=[
            pltpu.VMEM((tokens, features), F32),
            pltpu.VMEM((tokens, features), BF16),
            pltpu.VMEM((tokens, LANES), BF16),
            pltpu.VMEM((tokens, LANES), F32),
        ],
        compiler_params=params(),
        cost_estimate=pl.CostEstimate(flops=16 * LANES * tokens * features, bytes_accessed=8 * tokens * features, transcendentals=0),
        name="local_scan",
    )(doc_lengths, a_log, d_skip, held[0], b_sel, b_turned, held[1], x_in, held[2])


def one_language(first, size, starts, lang_ref):
    lang = lang_at(first, starts, lang_ref)
    same = jnp.bool_(True)
    for d, s in enumerate(starts):
        inside = (s > first) & (s < first + size)
        same = same & jnp.logical_not(inside & (lang_ref[d] != lang))
    return lang, same


def other_language(lang, first, size, starts, langs):
    other = lang
    few = jnp.bool_(True)
    for d, s in enumerate(starts):
        inside = (s > first) & (s < first + size) & (langs[d] != lang)
        few = few & jnp.logical_not(inside & (other != lang) & (langs[d] != other))
        other = jnp.where(inside & (other == lang), langs[d], other)
    return other, few


def has_language(which, first, size, starts, lang_ref):
    found = lang_at(first, starts, lang_ref) == which
    for d, s in enumerate(starts):
        found = found | ((s > first) & (s < first + size) & (lang_ref[d] == which))
    return found


def sum_rows(tile):
    return -(-8 * (tile // LANES) // 16) * 16


def combine_kernel(n_states, slot, tile_tokens, offset, len_ref, lang_ref, c_ref, reach_ref, part_ref, gate_ref, gain_ref, down_ref, *rest):
    states, (all_gated_ref, other_ref, mine_ref, enter_ref, low_ref) = rest[:n_states], rest[n_states:]
    step = pl.program_id(0)
    tokens, features = tile_tokens, part_ref.shape[1]
    heads = features // LANES
    tile = (step + 1 + lax.axis_index("head")) % 2
    at = pl.multiple_of(offset + tile * tokens, LANES)
    now = pl.ds(at, tokens)
    gated_ref = all_gated_ref.at[pl.ds(pl.multiple_of(tile * tokens, LANES), tokens)]
    first = lax.axis_index("seq") * part_ref.shape[0] + at
    starts = starts_of(len_ref)
    langs = [lang_ref[d] for d in range(lang_ref.shape[0])]
    lang, same = one_language(first, tokens, starts, langs)

    if n_states > 1:
        @pl.when(step == 0)
        def _():
            total = states[0][...].astype(F32)
            for more in states[1:]:
                total = total + more[...].astype(F32)
            enter_ref[...] = total.astype(BF16)
        entering = enter_ref
    else:
        entering = states[0]

    squares = jnp.zeros((tokens, LANES), F32)
    low = jnp.zeros((tokens, LANES), F32)
    c_low = c_ref[now, :]
    reach = reach_ref[now, :]
    pair = min(2, heads)
    for p in range(heads // pair):
        wide = slice(p * pair * LANES, (p + 1) * pair * LANES)
        both = dot(c_low, entering[:, wide])
        scaled = []
        for i in range(pair):
            h = p * pair + i
            here = slice(h * LANES, (h + 1) * LANES)
            entered = both[:, i * LANES:(i + 1) * LANES] * reach[:, 2 * slot + h:2 * slot + h + 1]
            gated = part_ref[now, here] + entered * gate_ref[now, here].astype(F32)
            squares = squares + gated * gated
            scaled.append((gated * gain_ref[:, here]).astype(BF16))
            gated_ref[:, here] = scaled[-1]
        low = low + dot(jnp.concatenate(scaled, axis=1), down_ref[lang, wide, :])
    low_ref[...] = low

    @pl.when(jnp.logical_not(same))
    def _():
        token_lang = lang_at(first + lax.broadcasted_iota(I32, (tokens, LANES), 0), starts, langs)
        for k in range(down_ref.shape[0]):
            @pl.when(has_language(k, first, tokens, starts, langs) & (lang != k))
            def _():
                low_ref[...] = jnp.where(token_lang == k, dot(gated_ref[...], down_ref[k]), low_ref[...])

    ones = jnp.ones((8, LANES), F32)
    sums = lax.dot_general(ones, squares, (((1,), (1,)), ((), ())), precision=lax.Precision.HIGHEST, preferred_element_type=F32)
    rows = [sums[:, c * LANES:(c + 1) * LANES] for c in range(tokens // LANES)]
    rows = jnp.concatenate(rows + rows[:1] * (sum_rows(tokens) // 8 - len(rows)), axis=0)

    def message(ref):
        ref[0:tokens, :] = low_ref[...].astype(BF16)
        ref[tokens:tokens + sum_rows(tokens), :] = rows.astype(BF16)

    @pl.when(step == 0)
    def _():
        message(other_ref)

    @pl.when(step == 1)
    def _():
        message(mine_ref)


def combine(docs, c_sel, reach, part, gate, gain, down, states, offset, tile, slot):
    features = part.shape[1]
    held = [pltpu.with_memory_space_constraint(v, pltpu.VMEM) for v in [gain, down] + states]
    return pl.pallas_call(
        functools.partial(combine_kernel, len(states), slot, tile, offset),
        grid_spec=pltpu.PrefetchScalarGridSpec(
            num_scalar_prefetch=2,
            grid=(2,),
            in_specs=[in_vmem()] * (6 + len(states)),
            out_specs=[in_vmem()] * 3,
            scratch_shapes=[
                pltpu.VMEM(states[0].shape, BF16),
                pltpu.VMEM((tile, LANES), F32),
            ],
        ),
        out_shape=[
            pltpu.VMEM((2 * tile, features), BF16),
            pltpu.VMEM((tile + sum_rows(tile), LANES), BF16),
            pltpu.VMEM((tile + sum_rows(tile), LANES), BF16),
        ],
        compiler_params=params(),
        name="combine",
    )(*docs, c_sel, reach, part, gate, *held)


def finish_kernel(tile, offset, all_tokens, all_features, len_ref, lang_ref, mine_ref, other_ref, all_gated_ref, up_ref, *rest):
    out_ref = rest[-1]
    step = pl.program_id(0)
    tokens, features = out_ref.shape
    per = tile // tokens
    inside = pl.multiple_of((step % per) * tokens, LANES)
    gated_ref = all_gated_ref.at[pl.ds(pl.multiple_of(step * tokens, LANES), tokens)]
    ranks = up_ref.shape[1]
    first = lax.axis_index("seq") * all_tokens + offset + step * tokens
    starts = starts_of(len_ref)
    langs = [lang_ref[d] for d in range(lang_ref.shape[0])]
    is_mine = (step // per) == lax.axis_index("head") % 2
    low = jnp.where(is_mine, mine_ref[pl.ds(inside, tokens), :].astype(F32), other_ref[pl.ds(inside, tokens), :].astype(F32))
    sums = pl.ds(tile, sum_rows(tile))
    sums = jnp.where(is_mine, mine_ref[sums, :].astype(F32), other_ref[sums, :].astype(F32))
    scale = lax.rsqrt(sums / all_features + EPS)
    scale = jnp.concatenate([scale] * (LANES // sum_rows(tile)), axis=0).T
    columns = []
    for c in range(tokens // LANES):
        column = scale[:, 8 * c:8 * c + 1]
        for q in range(1, per):
            k = 8 * (c + q * (tokens // LANES))
            column = jnp.where(step % per == q, scale[:, k:k + 1], column)
        columns.append(column)
    scale = jnp.concatenate(columns, axis=0)
    low = (low * scale).astype(BF16)
    lang, _ = one_language(first, tokens, starts, langs)
    other, few = other_language(lang, first, tokens, starts, langs)
    token_lang = lang_at(first + lax.broadcasted_iota(I32, (tokens, LANES), 0), starts, langs)
    zero = jnp.zeros((), BF16)
    piece = min(4 * LANES, features)

    @pl.when(few)
    def _():
        spread = jnp.concatenate([
            jnp.where(token_lang == lang, low, zero),
            jnp.where(token_lang != lang, low, zero),
        ], axis=1)
        for at in range(0, features, piece):
            here = slice(at, at + piece)
            lifted = dot(spread, jnp.concatenate([up_ref[lang, :, here], up_ref[other, :, here]], axis=0))
            out_ref[:, here] = (gated_ref[:, here].astype(F32) * scale + lifted).astype(BF16)

    @pl.when(jnp.logical_not(few))
    def _():
        spread = jnp.concatenate([jnp.where(token_lang == k, low, zero) for k in range(up_ref.shape[0])], axis=1)
        for at in range(0, features, piece):
            here = slice(at, at + piece)
            lifted = dot(spread, up_ref[:, :, here].reshape(up_ref.shape[0] * ranks, piece))
            out_ref[:, here] = (gated_ref[:, here].astype(F32) * scale + lifted).astype(BF16)


def finish(docs, mine, other, gated, up, offset, all_tokens, all_features, into=None):
    features = gated.shape[1]
    tile = gated.shape[0] // 2
    rows = next(r for r in (2 * LANES, LANES) if tile % r == 0 and offset % r == 0)
    held = [pltpu.with_memory_space_constraint(v, pltpu.VMEM) for v in (mine, other, gated, up)]
    more = [] if into is None else [into]
    return pl.pallas_call(
        functools.partial(finish_kernel, tile, offset, all_tokens, all_features),
        grid_spec=pltpu.PrefetchScalarGridSpec(
            num_scalar_prefetch=2,
            grid=(2 * tile // rows,),
            in_specs=[in_vmem()] * 4 + [pl.BlockSpec(memory_space=pl.ANY) for _ in more],
            out_specs=pl.BlockSpec((rows, features), lambda s, *_: (offset // rows + s, 0)),
        ),
        out_shape=jax.ShapeDtypeStruct((all_tokens, features), BF16),
        input_output_aliases={6: 0} if more else {},
        compiler_params=params(),
        name="finish",
    )(*docs, *held, *more)


def sum_over_head(other, mine, devices, beside=None):
    def across(v, mask):
        return lax.ppermute(v, "head", [(i, i ^ mask) for i in range(devices)])

    more = () if beside is None else (beside,)
    if devices == 1:
        return (mine, other) + more
    total = (mine.astype(F32) + across(other, 1).astype(F32)).astype(BF16)
    bit = 2
    while bit < devices:
        masks = [bit] if 2 * bit >= devices else [bit, 2 * bit, 3 * bit]
        arrived = [across(total, m) for m in masks]
        if bit == 2 and more:
            arrived, more = lax.optimization_barrier((arrived, more))
        added = total.astype(F32)
        for a in arrived:
            added = added + a.astype(F32)
        total = added.astype(BF16)
        bit *= 2 ** (1 if len(masks) == 1 else 2)
    return (total, across(total, 1)) + more


def run(seq_size, head_size, relayed, x_in, z_gate, b_input, c_input, dt_raw, a_log, d_skip, norm_gain,
        doc_lengths, doc_lang, adapt_down, adapt_up):
    tokens, features = x_in.shape
    heads = dt_raw.shape[0]
    groups = b_input.shape[1]
    b_rows = b_input.reshape(tokens * groups, b_input.shape[2])
    c_rows = c_input.reshape(tokens * groups, c_input.shape[2])
    docs = (doc_lengths, doc_lang)
    gain = norm_gain.reshape(1, features)
    all_features = features * head_size
    slot = max(8, heads)
    onward = [(i, i + 1) for i in range(seq_size - 1)]

    state, through, b_sel, b_turned, x_held = block_states(head_size, doc_lengths, a_log, dt_raw, b_rows, x_in)
    state, z_gate, c_rows = lax.optimization_barrier((state, z_gate, c_rows))
    arrived = lax.ppermute(state, "seq", onward)
    part, gate, c_sel, reach = local_scan(head_size, doc_lengths, a_log, d_skip, dt_raw, b_sel, b_turned, c_rows, x_held, z_gate)
    arrived, part = lax.optimization_barrier((arrived, part))
    states = [arrived]
    for _ in range(1, hops_of(tokens, seq_size) if relayed else 1):
        arrived = lax.ppermute((arrived.astype(F32) * through[0:1]).astype(BF16), "seq", onward)
        states.append(arrived)

    head = tokens
    if relayed:
        reached = longest_of(tokens, seq_size) - 1 - (len(states) - 1) * tokens
        head = next((h for h in (tokens // 4, tokens // 2) if reached <= h), tokens)

    def joined(states, offset, tile):
        return combine(docs, c_sel, reach, part, gate, gain, adapt_down, states, offset, tile, slot)

    if head == tokens:
        gated, other, mine = joined(states, 0, tokens // 2)
        sums = sum_over_head(other, mine, head_size)
        return finish(docs, *sums, gated, adapt_up, 0, tokens, all_features)
    late, other, mine = joined(states[:-1], head, (tokens - head) // 2)
    late_sums = sum_over_head(other, mine, head_size)
    states[-1], late_sums = lax.optimization_barrier((states[-1], late_sums))
    early, other, mine = joined(states, 0, head // 2)
    out = finish(docs, *late_sums, late, adapt_up, head, tokens, all_features)
    *early_sums, out = sum_over_head(other, mine, head_size, out)
    return finish(docs, *early_sums, early, adapt_up, 0, tokens, all_features, out)


def longest_of(tokens, seq_size):
    return tokens * seq_size // LONGEST_SHARE


def hops_of(tokens, seq_size):
    return min(-(-(longest_of(tokens, seq_size) - 1) // tokens), seq_size - 1)


def covered_kernel(tokens, seq_size, len_ref, out_ref):
    found, at = jnp.int32(0), jnp.int32(0)
    for d in range(len_ref.shape[0]):
        end = at + len_ref[d]
        for block in range(1, seq_size - 1):
            found = jnp.where((at < block * tokens) & (end > (block + 1) * tokens), 1, found)
        at = end
    out_ref[0] = found


def per_device(seq_size, head_size, *args):
    tokens = args[0].shape[0]
    doc_lengths = args[8]
    if hops_of(tokens, seq_size) < 2:
        return run(seq_size, head_size, False, *args)
    covered = pl.pallas_call(
        functools.partial(covered_kernel, tokens, seq_size),
        in_specs=[pl.BlockSpec(memory_space=pltpu.SMEM)],
        out_specs=pl.BlockSpec(memory_space=pltpu.SMEM),
        out_shape=jax.ShapeDtypeStruct((1,), I32),
        name="covered",
    )(doc_lengths)[0] > 0
    return lax.cond(
        covered,
        functools.partial(run, seq_size, head_size, True),
        functools.partial(run, seq_size, head_size, False),
        *args,
    )


def solution(mesh):
    placed = (
        P("seq", "head"),
        P("seq", "head"),
        P("seq", None, None),
        P("seq", None, None),
        P("head", "seq"),
        P("head"),
        P("head"),
        P("head"),
        P(),
        P(),
        P(None, "head", None),
        P(None, None, "head"),
    )
    return jax.shard_map(
        functools.partial(per_device, mesh.shape["seq"], mesh.shape["head"]),
        mesh=mesh, in_specs=placed, out_specs=P("seq", "head"), check_vma=False,
    )
```

time: 63.7 us -> 47.4 us (0.74)
  starting transfers between devices: 16 us -> 8.66 us
  Pallas kernels: 34.7 us -> 27.4 us
  waiting for transfers between devices: 10.6 us -> 9.35 us
  other arithmetic: 1.08 us -> 0.12 us
  local copies, waits for them, and re-layouts: 0.7 us -> 0.06 us
    pallas_call x6 -> x5, Pallas kernels: 34.7 us -> 27.4 us  [the longest x1 10.6 us: local_scan(): pl.pallas_call(functools.partial(scan_kernel, head_size), grid_spec=pltpu...]
    ppermute x2 -> x1, waiting for transfers between devices: 6.98 us -> 0.44 us  [run(): arrived = lax.ppermute(state, 'seq', onward)]
    ppermute x10 -> x5, waiting for transfers between devices: 3.67 us -> 8.91 us  [across(): return lax.ppermute(v, 'head', [(i, i ^ mask) for i in range(devices)])]
    ppermute x10 -> x5, starting transfers between devices: 7.39 us -> 3.7 us  [across(): return lax.ppermute(v, 'head', [(i, i ^ mask) for i in range(devices)])]
    ppermute x2 -> x1, starting transfers between devices: 8.63 us -> 4.96 us  [run(): arrived = lax.ppermute(state, 'seq', onward)]
    concatenate x1 -> x0, other arithmetic: 0.78 us -> none  [per_device(): docs = jnp.concatenate([doc_lengths, doc_lang])]
    unnamed x16 -> x0, local copies, waits for them, and re-layouts: 0.69 us -> none
  transfers between devices with their start and end apart: 12 -> 6, of which waited for: 5 -> 6; matrix products, arithmetic and copies ran while one was open for 0% -> 0% of each run, Pallas kernels for 40% -> 23%
where the time goes in v3:
time: 47.4 us; the launch traced here: 46.5 us
  Pallas kernels  27.4 us (58%)
  waiting for transfers between devices  9.35 us (20%)
  starting transfers between devices  8.66 us (18%)
  between operations  0.66 us (1%)
    pallas_call x1, Pallas kernels, local_scan(): pl.pallas_call(functools.partial(scan_kernel, head_size), grid_spec=pltpu...  10.6 us
    ppermute x5, waiting for transfers between devices, across(): return lax.ppermute(v, 'head', [(i, i ^ mask) for i in range(devices)])  8.91 us
    pallas_call x1, Pallas kernels, combine(): pl.pallas_call(functools.partial(combine_kernel, len(states), slot, tile,...  5.62 us
    pallas_call x1, Pallas kernels, finish(): pl.pallas_call(functools.partial(finish_kernel, tile, offset, all_tokens,...  5.02 us
    pallas_call x1, Pallas kernels, block_states(): pl.pallas_call(functools.partial(state_kernel, head_size), grid_spec=pltp...  4.99 us
    ppermute x1, starting transfers between devices, run(): arrived = lax.ppermute(state, 'seq', onward)  4.96 us
    ppermute x5, starting transfers between devices, across(): return lax.ppermute(v, 'head', [(i, i ^ mask) for i in range(devices)])  3.7 us
    pallas_call x1, Pallas kernels, per_device(): pl.pallas_call(functools.partial(covered_kernel, tokens, seq_size), in_sp...  1.2 us
  transfers between devices with their start and end apart: 6, of which 6 were waited for; matrix products, arithmetic and copies ran while one was open for 0% of the time, Pallas kernels for 23%

profile of v3, /device:TPU:0, one launch (start us, length us, event | category | flops | bytes accessed | tf_op | source)
XLA Modules:
  0.0 46.5 jit_solution(16284174769404461425)
XLA Ops:
  0.0 1.2 %covered.1 = s32[1]{0:T(128)} custom-call(s32[6]{0:T(128)} %len_ref.1), custom_call_target="tpu_custom_call" | custom-call | tf_op jit(solution)/shard_map/covered/pallas_call | solution.py:566
  1.9 44.6 %conditional.1 = (bf16[1024,2048]{1,0:T(8,128)(2,1)}) conditional(s32[]{:T(128)} %bitcast.7, (bf16[1024,8,128]{2,1,0:T(8,128)(2,1)}, s32[6]{0:T(128)}, f32[16]{0:T(128)}, f32[16,1024]{1,0:T(8,128)}, bf16[1024,2048]{1,0:T(8,128)(2,1)}, /*index=5*/bf16[1024,8,128]{2,1,0:T(8,128)(2,1)}, bf16[1024,2048]{1,0:T(8,128)(2,1)}, f32[16]{0:T(128)}, ...), branch_computations={%region_0.0_spmd, %region_1.0_spmd} | conditional | flops 4833460224 | bytes 84960712 | solution.py:573
  1.9 0.0 copy-start.4
  1.9 0.0 copy-start.8
  1.9 0.0 copy-start.10
  1.9 0.0 copy-start.12
  1.9 0.0 copy-start.16
  1.9 0.0 copy-start.18
  1.9 5.0 %block_states.2 = (bf16[128,2048]{1,0:T(8,128)(2,1)S(1)}, f32[8,2048]{1,0:T(8,128)}, bf16[1024,128]{1,0:T(8,128)(2,1)S(1)}, bf16[128,1024]{1,0:T(8,128)(2,1)S(1)}, bf16[1024,2048]{1,0:T(8,128)(2,1)S(1)}) custom-call(s32[6]{0:T(128)} %get-tuple-element.56.len_hbm.len_ref, f32[16]{0:T(128)} %get-tuple-element.58.alog_hbm.alog_ref, ...), custom_call_target="tpu_custom_call" | custom-call | flops 536870912 | bytes 16777216 | tf_op jit(solution)/shard_map/cond/branch_0_fun/block_states/pallas_call | solution.py:147
  6.9 5.0 %collective-permute-start = (bf16[128,2048]{1,0:T(8,128)(2,1)S(1)}, bf16[128,2048]{1,0:T(8,128)(2,1)S(1)}, u32[]{:S(2)}, u32[]{:S(2)}) collective-permute-start(bf16[128,2048]{1,0:T(8,128)(2,1)S(1)} %get-tuple-element.73), channel_id=1, source_target_pairs={{0,8},{8,16},{16,24},{1,9},{9,17},{17,25},{2,10},{10,18},{18,26},{... | collective-permute-start | bytes 1572872 | tf_op jit(solution)/shard_map/cond/branch_0_fun/ppermute | solution.py:514
  11.9 0.0 copy-done.4
  11.9 0.0 copy-done.8
  11.9 0.0 copy-done.10
  11.9 0.0 copy-done.12
  12.0 0.0 copy-start
  12.0 0.0 copy-start.6
  12.0 0.0 copy-start.14
  12.0 10.6 %local_scan.2 = (f32[1024,2048]{1,0:T(8,128)S(1)}, bf16[1024,2048]{1,0:T(8,128)(2,1)S(1)}, bf16[1024,128]{1,0:T(8,128)(2,1)S(1)}, f32[1024,128]{1,0:T(8,128)S(1)}) custom-call(s32[6]{0:T(128)S(1)} %copy-done.12, f32[16]{0:T(128)S(1)} %copy-done.16, f32[16]{0:T(128)S(1)} %copy-done.18, f32[16,1024]{1,0:T(8,128)S(1)} %copy-done.4, ...), custom_call_target="tpu_custom_call" | custom-call | flops 4294967296 | bytes 16777216 | tf_op jit(solution)/shard_map/cond/branch_0_fun/local_scan/pallas_call | solution.py:250
  22.6 0.4 collective-permute-done.rest_0_
  23.0 5.6 %combine.3 = (bf16[1024,2048]{1,0:T(8,128)(2,1)S(1)}, bf16[544,128]{1,0:T(8,128)(2,1)S(1)}, bf16[544,128]{1,0:T(8,128)(2,1)S(1)}) custom-call(s32[6]{0:T(128)S(1)} %copy-done.12, s32[6]{0:T(128)S(1)} %copy-done.14, bf16[1024,128]{1,0:T(8,128)(2,1)S(1)} %get-tuple-element.71.c_ref, f32[1024,128]{1,0:T(8,128)S(1)} %get-tuple-element.72.reach_ref, ...), custom_call_target="tpu_custom_call" | custom-call | tf_op jit(solution)/shard_map/cond/branch_0_fun/combine/pallas_call | solution.py:382
  28.7 0.1 collective-permute-start.1
  28.8 1.3 %collective-permute-done.1 = bf16[544,128]{1,0:T(8,128)(2,1)S(1)} collective-permute-done((bf16[544,128]{1,0:T(8,128)(2,1)S(1)}, bf16[544,128]{1,0:T(8,128)(2,1)S(1)}, u32[]{:S(2)}, u32[]{:S(2)}) %collective-permute-start.1) | collective-permute-done | bytes 139296 | tf_op jit(solution)/shard_map/cond/branch_0_fun/ppermute | solution.py:479
  30.1 2.5 %collective-permute-start.4 = (bf16[544,128]{1,0:T(8,128)(2,1)S(1)}, bf16[544,128]{1,0:T(8,128)(2,1)S(1)}, u32[]{:S(2)}, u32[]{:S(2)}) collective-permute-start(bf16[544,128]{1,0:T(8,128)(2,1)S(1)} %add_convert_fusion.1), channel_id=1, source_target_pairs={{0,6},{1,7},{2,4},{3,5},{4,2},{5,3},{6,0},{7,1},{8,14},{9,15},{10,... | collective-permute-start | bytes 417800 | tf_op jit(solution)/shard_map/cond/branch_0_fun/ppermute | solution.py:479
  32.7 0.5 %collective-permute-start.3 = (bf16[544,128]{1,0:T(8,128)(2,1)S(1)}, bf16[544,128]{1,0:T(8,128)(2,1)S(1)}, u32[]{:S(2)}, u32[]{:S(2)}) collective-permute-start(bf16[544,128]{1,0:T(8,128)(2,1)S(1)} %add_convert_fusion.1), channel_id=1, source_target_pairs={{0,4},{1,5},{2,6},{3,7},{4,0},{5,1},{6,2},{7,3},{8,12},{9,13},{10,... | collective-permute-start | bytes 417800 | tf_op jit(solution)/shard_map/cond/branch_0_fun/ppermute | solution.py:479
  33.2 0.5 %collective-permute-start.2 = (bf16[544,128]{1,0:T(8,128)(2,1)S(1)}, bf16[544,128]{1,0:T(8,128)(2,1)S(1)}, u32[]{:S(2)}, u32[]{:S(2)}) collective-permute-start(bf16[544,128]{1,0:T(8,128)(2,1)S(1)} %add_convert_fusion.1), channel_id=1, source_target_pairs={{0,2},{1,3},{2,0},{3,1},{4,6},{5,7},{6,4},{7,5},{8,10},{9,11},{10,... | collective-permute-start | bytes 417800 | tf_op jit(solution)/shard_map/cond/branch_0_fun/ppermute | solution.py:479
  33.7 3.6 %collective-permute-done.4 = bf16[544,128]{1,0:T(8,128)(2,1)S(1)} collective-permute-done((bf16[544,128]{1,0:T(8,128)(2,1)S(1)}, bf16[544,128]{1,0:T(8,128)(2,1)S(1)}, u32[]{:S(2)}, u32[]{:S(2)}) %collective-permute-start.4) | collective-permute-done | bytes 139296 | tf_op jit(solution)/shard_map/cond/branch_0_fun/ppermute | solution.py:479
  37.3 2.5 %collective-permute-done.3 = bf16[544,128]{1,0:T(8,128)(2,1)S(1)} collective-permute-done((bf16[544,128]{1,0:T(8,128)(2,1)S(1)}, bf16[544,128]{1,0:T(8,128)(2,1)S(1)}, u32[]{:S(2)}, u32[]{:S(2)}) %collective-permute-start.3) | collective-permute-done | bytes 139296 | tf_op jit(solution)/shard_map/cond/branch_0_fun/ppermute | solution.py:479
  39.8 0.1 collective-permute-done.2
  39.9 0.1 add_convert_fusion.mine_ref
  40.0 0.1 collective-permute-start.5
  40.1 1.3 %collective-permute-done.5.other_ref = bf16[544,128]{1,0:T(8,128)(2,1)S(1)} collective-permute-done((bf16[544,128]{1,0:T(8,128)(2,1)S(1)}, bf16[544,128]{1,0:T(8,128)(2,1)S(1)}, u32[]{:S(2)}, u32[]{:S(2)}) %collective-permute-start.5) | collective-permute-done | bytes 139296 | tf_op jit(solution)/shard_map/cond/branch_0_fun/ppermute | solution.py:479
  41.4 5.0 %finish.3 = bf16[1024,2048]{1,0:T(8,128)(2,1)} custom-call(s32[6]{0:T(128)S(1)} %copy-done.12, s32[6]{0:T(128)S(1)} %copy-done.14, bf16[544,128]{1,0:T(8,128)(2,1)S(1)} %add_convert_fusion.mine_ref, bf16[544,128]{1,0:T(8,128)(2,1)S(1)} %collective-permute-done.5.other_ref, bf16[1024,2048]{1,0:T(8,128)(2,1)S(1)} %get-tuple-element.82.all_gated_ref, ...), custom_call_target="tpu_custom_call" | custom-call | tf_op jit(solution)/shard_map/cond/branch_0_fun/finish/pallas_call | solution.py:462
  (8 shorter events, 0.1 us)
Async XLA Ops:
  1.9 10.0 %copy-start.4 = (f32[16,1024]{1,0:T(8,128)S(1)}, f32[16,1024]{1,0:T(8,128)}, u32[]{:S(2)}) copy-start(f32[16,1024]{1,0:T(8,128)} %get-tuple-element.60.dt_hbm.dt_ref) | copy-start | bytes 196612 | tf_op jit(solution)/shard_map/cond
  1.9 10.0 %copy-start.8 = (bf16[1024,2048]{1,0:T(8,128)(2,1)S(1)}, bf16[1024,2048]{1,0:T(8,128)(2,1)}, u32[]{:S(2)}) copy-start(bf16[1024,2048]{1,0:T(8,128)(2,1)} %get-tuple-element.70.z_ref) | copy-start | bytes 12582916 | tf_op jit(solution)/shard_map/cond
  1.9 10.0 %copy-start.10 = (bf16[1024,8,128]{2,1,0:T(8,128)(2,1)S(1)}, bf16[1024,8,128]{2,1,0:T(8,128)(2,1)}, u32[]{:S(2)}) copy-start(bf16[1024,8,128]{2,1,0:T(8,128)(2,1)} %get-tuple-element.67) | copy-start | bytes 6291460 | tf_op jit(solution)/shard_map/cond
  1.9 10.0 %copy-start.12 = (s32[6]{0:T(128)S(1)}, s32[6]{0:T(128)}, u32[]{:S(2)}) copy-start(s32[6]{0:T(128)} %get-tuple-element.56.len_hbm.len_ref) | copy-start | bytes 76 | tf_op jit(solution)/shard_map/cond
  1.9 10.0 %copy-start.16 = (f32[16]{0:T(128)S(1)}, f32[16]{0:T(128)}, u32[]{:S(2)}) copy-start(f32[16]{0:T(128)} %get-tuple-element.58.alog_hbm.alog_ref) | copy-start | bytes 196 | tf_op jit(solution)/shard_map/cond
  1.9 10.0 %copy-start.18 = (f32[16]{0:T(128)S(1)}, f32[16]{0:T(128)}, u32[]{:S(2)}) copy-start(f32[16]{0:T(128)} %get-tuple-element.59.skip_ref) | copy-start | bytes 196 | tf_op jit(solution)/shard_map/cond
  6.9 16.1 %collective-permute-start = (bf16[128,2048]{1,0:T(8,128)(2,1)S(1)}, bf16[128,2048]{1,0:T(8,128)(2,1)S(1)}, u32[]{:S(2)}, u32[]{:S(2)}) collective-permute-start(bf16[128,2048]{1,0:T(8,128)(2,1)S(1)} %get-tuple-element.73), channel_id=1, source_target_pairs={{0,8},{8,16},{16,24},{1,9},{9,17},{17,25},{2,10},{10,18},{18,26},{... | collective-permute-start | bytes 1572872 | tf_op jit(solution)/shard_map/cond/branch_0_fun/ppermute | solution.py:514
  12.0 11.1 %copy-start = (bf16[4,2048,128]{2,1,0:T(8,128)(2,1)S(1)}, bf16[4,2048,128]{2,1,0:T(8,128)(2,1)}, u32[]{:S(2)}) copy-start(bf16[4,2048,128]{2,1,0:T(8,128)(2,1)} %get-tuple-element.78.down_ref) | copy-start | bytes 6291460 | tf_op jit(solution)/shard_map/cond
  12.0 11.1 %copy-start.6 = (f32[2048]{0:T(1024)S(1)}, f32[2048]{0:T(1024)}, u32[]{:S(2)}) copy-start(f32[2048]{0:T(1024)} %get-tuple-element.77) | copy-start | bytes 24580 | tf_op jit(solution)/shard_map/cond
  12.0 11.1 %copy-start.14 = (s32[6]{0:T(128)S(1)}, s32[6]{0:T(128)}, u32[]{:S(2)}) copy-start(s32[6]{0:T(128)} %get-tuple-element.57.lang_ref) | copy-start | bytes 76 | tf_op jit(solution)/shard_map/cond
  23.0 18.4 %copy-start.2 = (bf16[4,128,2048]{2,1,0:T(8,128)(2,1)S(1)}, bf16[4,128,2048]{2,1,0:T(8,128)(2,1)}, u32[]{:S(2)}) copy-start(bf16[4,128,2048]{2,1,0:T(8,128)(2,1)} %get-tuple-element.83.up_ref) | copy-start | bytes 6291460 | tf_op jit(solution)/shard_map/cond
  28.7 1.4 %collective-permute-start.1 = (bf16[544,128]{1,0:T(8,128)(2,1)S(1)}, bf16[544,128]{1,0:T(8,128)(2,1)S(1)}, u32[]{:S(2)}, u32[]{:S(2)}) collective-permute-start(bf16[544,128]{1,0:T(8,128)(2,1)S(1)} %get-tuple-element.81), channel_id=1, source_target_pairs={{0,1},{1,0},{2,3},{3,2},{4,5},{5,4},{6,7},{7,6},{8,9},{9,8},{10,11... | collective-permute-start | bytes 417800 | tf_op jit(solution)/shard_map/cond/branch_0_fun/ppermute | solution.py:479
  30.1 7.2 %collective-permute-start.4 = (bf16[544,128]{1,0:T(8,128)(2,1)S(1)}, bf16[544,128]{1,0:T(8,128)(2,1)S(1)}, u32[]{:S(2)}, u32[]{:S(2)}) collective-permute-start(bf16[544,128]{1,0:T(8,128)(2,1)S(1)} %add_convert_fusion.1), channel_id=1, source_target_pairs={{0,6},{1,7},{2,4},{3,5},{4,2},{5,3},{6,0},{7,1},{8,14},{9,15},{10,... | collective-permute-start | bytes 417800 | tf_op jit(solution)/shard_map/cond/branch_0_fun/ppermute | solution.py:479
  32.7 7.2 %collective-permute-start.3 = (bf16[544,128]{1,0:T(8,128)(2,1)S(1)}, bf16[544,128]{1,0:T(8,128)(2,1)S(1)}, u32[]{:S(2)}, u32[]{:S(2)}) collective-permute-start(bf16[544,128]{1,0:T(8,128)(2,1)S(1)} %add_convert_fusion.1), channel_id=1, source_target_pairs={{0,4},{1,5},{2,6},{3,7},{4,0},{5,1},{6,2},{7,3},{8,12},{9,13},{10,... | collective-permute-start | bytes 417800 | tf_op jit(solution)/shard_map/cond/branch_0_fun/ppermute | solution.py:479
  33.2 6.8 %collective-permute-start.2 = (bf16[544,128]{1,0:T(8,128)(2,1)S(1)}, bf16[544,128]{1,0:T(8,128)(2,1)S(1)}, u32[]{:S(2)}, u32[]{:S(2)}) collective-permute-start(bf16[544,128]{1,0:T(8,128)(2,1)S(1)} %add_convert_fusion.1), channel_id=1, source_target_pairs={{0,2},{1,3},{2,0},{3,1},{4,6},{5,7},{6,4},{7,5},{8,10},{9,11},{10,... | collective-permute-start | bytes 417800 | tf_op jit(solution)/shard_map/cond/branch_0_fun/ppermute | solution.py:479
  40.0 1.4 %collective-permute-start.5 = (bf16[544,128]{1,0:T(8,128)(2,1)S(1)}, bf16[544,128]{1,0:T(8,128)(2,1)S(1)}, u32[]{:S(2)}, u32[]{:S(2)}) collective-permute-start(bf16[544,128]{1,0:T(8,128)(2,1)S(1)} %add_convert_fusion.mine_ref), channel_id=1, source_target_pairs={{0,1},{1,0},{2,3},{3,2},{4,5},{5,4},{6,7},{7,6},{8,9},{9,8},{10,11... | collective-permute-start | bytes 417800 | tf_op jit(solution)/shard_map/cond/branch_0_fun/ppermute | solution.py:479
